TPU v7x, 256 devices: a whole 4x4x8 slice. The times are simulated.
256 devices in a mesh: head: 8 (over z), rep: 32 (over x, y, core).
Axes of the slice: x: 4, y: 4, z: 8, core: 2. Of those that a mesh axis runs over, the one named last changes fastest.
Arguments:
- trainer_rows: bfloat16 [8, 32, 8, 8, 1024], P('head', 'rep'), may hold values from -2.5 to 2.5
- route: int32 [8, 32, 8, 2], replicated, may hold values from 0 to 2040, as said below
Outputs:
- absorbed_values: bfloat16 [64, 1536, 512], P('head')
- absorbed_scales: bfloat16 [64, 12, 4], P('head')
Inputs may be any that keep to these rules, and one draw needn't show every extreme that they name: route[i, j, s] holds the owner group (first entry) and the row offset (second entry) of slot s of the trainer shard on head index i and replica j. The owner groups of one shard's 8 slots are all different; for each owner group the offsets of its 256 slots are the multiples of 8 below 2048, each once.
All inputs are finite; a program needn't handle non-finite values. Where the computation divides by a largest or mean magnitude, that divisor is 1e-20 or more.
Results may differ from a plain program's by a relative error of at most 0.013.
Values may be sent and summed in bfloat16 or wider, within the bound.
No kernel may reach another device: no remote copies, remote signals or barrier semaphores. Data moves between devices by JAX's collectives and lax.ppermute only.
A program may use at most 128 MiB of HBM per device.

v0:
```python
import jax
import jax.numpy as jnp
from jax import lax
from jax.sharding import PartitionSpec as P

QR = 1536
KR = 512
DH = 128
H_DEV = 8
QB = 128


EPSILON = 1e-06


def absorb(query_heads, key_heads):
    products = jnp.einsum(
        "hqd,hkd->hqk", query_heads, key_heads, preferred_element_type=jnp.float32
    )
    head_count, row_count, col_count = products.shape
    row_blocks = row_count // QB
    col_blocks = col_count // QB
    banded = jnp.abs(products).reshape(head_count, row_blocks, QB, col_count)
    row_peak = jnp.max(banded, axis=2)
    peaks = jnp.max(row_peak.reshape(head_count, row_blocks, col_blocks, QB), axis=3)
    scales = (peaks + EPSILON).astype(jnp.bfloat16)
    spread = jnp.repeat(scales.astype(jnp.float32), QB, axis=2)
    values = (
        products.reshape(head_count, row_blocks, QB, col_count) / spread[:, :, None, :]
    ).astype(jnp.bfloat16)
    return (values.reshape(head_count, row_count, col_count), scales)


def source_order(order_offsets, block_rows):
    count = order_offsets.shape[0]
    positions = jnp.arange(count, dtype=jnp.int32)
    targets = order_offsets // block_rows
    matches = targets[None, :] == positions[:, None]
    return jnp.sum(jnp.where(matches, positions[None, :], 0), axis=1)


def place(blocks, sources, total):
    taken = jnp.take(blocks, sources, axis=0)
    return taken.reshape((total,) + blocks.shape[2:])


def to_owners(ordered):
    return lax.all_to_all(ordered, "head", split_axis=0, concat_axis=0, tiled=True)


def split_heads(factors, total):
    stacked = factors.reshape(total, H_DEV, DH).transpose(1, 0, 2)
    return (stacked[:, :QR], stacked[:, QR:])


def on_device(trainer_rows, route):
    group = lax.axis_index("head")
    replica = lax.axis_index("rep")
    held = trainer_rows[0, 0]
    slot_count = held.shape[0]
    block_rows = held.shape[1]
    total = QR + KR
    own_slots = route[group, replica, :, 0]
    slot_ids = jnp.arange(slot_count, dtype=jnp.int32)
    matches = own_slots[None, :] == slot_ids[:, None]
    picks = jnp.sum(jnp.where(matches, slot_ids[None, :], 0), axis=1)
    ordered = held[picks]
    mine = route[:, :, :, 0] == group
    table = jnp.sum(jnp.where(mine, route[:, :, :, 1], 0), axis=2)
    order_offsets = table.T.reshape(-1)
    sources = source_order(order_offsets, block_rows)
    arrived = to_owners(ordered)
    everything = lax.all_gather(arrived, "rep", axis=0, tiled=True)
    factors = place(everything, sources, total)
    query_heads, key_heads = split_heads(factors, total)
    values, scales = absorb(query_heads, key_heads)
    return (values, scales)


def solution(mesh):
    placed = (P("head", "rep", None, None, None), P())
    return jax.shard_map(
        on_device,
        mesh=mesh,
        in_specs=placed,
        out_specs=(P("head", None, None), P("head", None, None)),
        check_vma=False,
    )
```

profile of v0, /device:TPU:1, one launch (start us, length us, event | category | flops | bytes accessed | tf_op | source)
XLA Modules:
  0.0 139.4 jit_solution(13166536830463822481)
XLA Ops:
  7.2 0.0 copy-start
  7.2 0.0 all-gather.2.cloned.1.call-start
  7.2 1.0 dynamic-slice_reduce_fusion
  8.2 0.1 select_reduce_fusion.1
  8.4 0.6 gather_fusion
  9.0 16.7 %all_to_all.5 = bf16[8,8,1024]{2,1,0:T(8,128)(2,1)} all-to-all(bf16[8,8,1024]{2,1,0:T(8,128)(2,1)S(1)} %gather_fusion), channel_id=1, replica_groups=mesh['head'=8,'rep'=32] {'head'}, dimensions={0} | all-to-all | bytes 262144 | tf_op jit(solution)/shard_map/all_to_all | solution.py:48
  25.6 0.0 all-gather.2.cloned.1.call-update
  25.7 1.0 fusion.5
  26.7 0.1 copy.13
  26.7 0.1 reshape.83
  26.8 0.1 select_reduce_fusion
  27.0 0.1 broadcast_in_dim.54
  27.1 0.1 broadcast_in_dim.55
  27.2 48.1 %all-gather.2.cloned.1.call-done = bf16[256,8,1024]{2,1,0:T(8,128)(2,1)} async-done(((bf16[8,8,1024]{2,1,0:T(8,128)(2,1)}), bf16[256,8,1024]{2,1,0:T(8,128)(2,1)}) %all-gather.2.cloned.1.call-update) | async-done | bytes 4194320 | tf_op jit(solution)/shard_map/all_gather | solution.py:73
  75.3 5.0 %gather_fusion.1 = bf16[256,8,1024]{2,1,0:T(8,128)(2,1)} fusion(bf16[256,8,1024]{2,1,0:T(8,128)(2,1)} %all-gather.2.cloned.1.call-done, s32[1024]{0:T(1024)S(1)} %pad_clamp_fusion), kind=kCustom, calls=%fused_computation.1 | custom fusion | bytes 8389632 | tf_op jit(solution)/shard_map/jit(_take)/gather | solution.py:43
  80.3 3.3 %copy.18 = bf16[256,8,8,128]{3,2,1,0:T(8,128)(2,1)S(1)} copy(bf16[256,8,8,128]{3,1,2,0:T(8,128)(2,1)} %bitcast.25) | data formatting | bytes 8388608
  83.6 2.5 %fusion.1 = bf16[8,2048,128]{2,1,0:T(8,128)(2,1)} fusion(bf16[2048,8,128]{2,1,0:T(8,128)(2,1)S(1)} %bitcast.24, pred[2048]{0:T(1024)(128)(4,1)S(1)} %broadcast_in_dim.55), kind=kLoop, calls=%fused_computation.5 | loop fusion | flops 2097152 | bytes 8390656 | tf_op jit(solution)/shard_map/transpose | solution.py:52
  86.0 21.5 %fusion.8 = (f32[8,1536,512]{2,1,0:T(8,128)}, f32[8,1536,512]{2,1,0:T(8,128)}) fusion(bf16[8,2048,128]{2,1,0:T(8,128)(2,1)} %fusion.1), kind=kOutput, calls=%fused_computation.31 | convolution fusion | flops 1616904192 | bytes 54525952 | tf_op jit(solution)/shard_map/hqd,hkd->hqk/dot_general | solution.py:17
  107.5 9.8 %reduce_max.18 = f32[8,12,512]{2,1,0:T(8,128)S(1)} reduce(f32[8,12,128,512]{3,2,1,0:T(8,128)} %bitcast.23, f32[]{:T(128)} %constant.48.clone.1), dimensions={2}, to_apply=%region_3.4 | reduce | flops 6242304 | bytes 25362436 | tf_op jit(solution)/shard_map/reduce_max | solution.py:24
  117.3 0.2 bitcast_reduce_fusion
  117.5 0.7 copy.17
  118.2 0.1 broadcast_bitcast_fusion
  118.3 0.1 copy.16
  118.5 14.1 %fusion = bf16[8,1536,512]{2,1,0:T(8,128)(2,1)} fusion(f32[8,1536,512]{2,1,0:T(8,128)} %get-tuple-element.9, f32[8,12,512]{2,1,0:T(8,128)S(1)} %copy.16), kind=kLoop, calls=%fused_computation.3 | loop fusion | flops 12582912 | bytes 37945344 | tf_op jit(solution)/shard_map/convert_element_type | solution.py:30
  (10 shorter events, 0.1 us)
Async XLA Ops:
  7.2 1.2 copy-start
  7.2 68.1 %all-gather.2.cloned.1.call-start = ((), (), s32[]{:S(2)}) async-start(), calls=%async_computation.1 | async-start | bytes 4325376 | tf_op jit(solution)/shard_map/all_gather | solution.py:73
  118.5 14.1 %copy-start.1 = (bf16[1,1,8,8,1024]{4,3,2,1,0:T(8,128)(2,1)S(1)}, bf16[1,1,8,8,1024]{4,3,2,1,0:T(8,128)(2,1)}, u32[]{:S(2)}) copy-start(bf16[1,1,8,8,1024]{4,3,2,1,0:T(8,128)(2,1)} %param.2) | copy-start | bytes 393220
Sparse Core Ops, SparseCore 0:
  25.8 49.4 all-gather.1
where the time goes:
time: 140 us; the launch traced here: 139 us
  waiting for transfers between devices  48.1 us (34%)
  other arithmetic  27.8 us (20%)
  matrix products  21.5 us (15%)
  blocking collectives  16.7 us (12%)
  between operations  14.2 us (10%)
  local copies, waits for them, and re-layouts  11.2 us (8%)
    all_gather x1, waiting for transfers between devices, on_device(): everything = lax.all_gather(arrived, 'rep', axis=0, tiled=True)  48.1 us
    dot_general x1, matrix products, absorb(): jnp.einsum('hqd,hkd->hqk', query_heads, key_heads, preferred_element_type...  21.5 us
    all_to_all x1, blocking collectives, to_owners(): lax.all_to_all(ordered, 'head', split_axis=0, concat_axis=0, tiled=True)  16.7 us
    convert_element_type x1, other arithmetic, absorb(): values = (products.reshape(head_count, row_blocks, QB, col_count) / sprea...  14.1 us
    reduce_max x1, other arithmetic, absorb(): row_peak = jnp.max(banded, axis=2)  9.79 us
    gather x1, local copies, waits for them, and re-layouts, place(): taken = jnp.take(blocks, sources, axis=0)  5.02 us
    unnamed x6, local copies, waits for them, and re-layouts  4 us
  transfers between devices with their start and end apart: 1, of which 1 were waited for; matrix products, arithmetic and copies ran while one was open for 1% of the time, Pallas kernels for 0%

commit v1 on v0

v1 whole, which is shorter than its diff:
```python
import functools

import jax
import jax.numpy as jnp
from jax import lax
from jax.experimental import pallas as pl
from jax.experimental.pallas import tpu as pltpu
from jax.sharding import PartitionSpec as P

QR = 1536
KR = 512
DH = 128
H_DEV = 8
QB = 128
LAT = QR + KR
NZ = 8
NX = 4
NY = 4
NC = 2
HALF = H_DEV // NC
WIDE = HALF * DH
EPSILON = 1e-06
AXES = ("head", "rep")


def index_of(z, x, y, c):
    return (z % NZ) * (NX * NY * NC) + (x % NX) * (NY * NC) + (y % NY) * NC + c


def every():
    return [
        (z, x, y, c)
        for z in range(NZ)
        for x in range(NX)
        for y in range(NY)
        for c in range(NC)
    ]


def pairs(target):
    return [(index_of(*d), index_of(*target(*d))) for d in every()]


def first_axis(k):
    return pairs(lambda z, x, y, c: (z, x - k, y, c) if c == 0 else (z, x, y - k, c))


def second_axis(k):
    return pairs(lambda z, x, y, c: (z, x, y - k, c) if c == 0 else (z, x - k, y, c))


def other_core():
    return pairs(lambda z, x, y, c: (z, x, y, 1 - c))


def columns():
    return [
        [index_of(z, x, y, c) for z in range(NZ) for c in range(NC)]
        for x in range(NX)
        for y in range(NY)
    ]


def absorb_kernel(swapped, meta, rows, b0, b1, b2, b3, *refs):
    values, scales, placed = refs[-3:]
    step = pl.program_id(0)

    @pl.when(step == 0)
    def _():
        swap = meta[0] if not swapped else 1 - meta[0]
        at_x, at_y = meta[1], meta[2]
        for second, blocks in enumerate((b0, b1, b2, b3)):

            def body(first, carry, second=second, blocks=blocks):
                x = (at_x + jnp.where(swap == 1, second, first)) & (NX - 1)
                y = (at_y + jnp.where(swap == 1, first, second)) & (NY - 1)
                for z in range(NZ):
                    for c in range(NC):
                        row = pl.multiple_of(rows[z, x * (NY * NC) + y * NC + c], 8)
                        block = blocks[first * (NZ * NC) + z * NC + c].astype(jnp.float32)
                        for h in range(HALF):
                            placed[h, pl.ds(row, 8), :] = block[:, h * DH : (h + 1) * DH]
                return carry

            lax.fori_loop(0, NX, body, 0)

    key = placed[step, QR:, :].astype(jnp.bfloat16)
    row_at = lax.broadcasted_iota(jnp.int32, (4, 128), 0)
    col_at = lax.broadcasted_iota(jnp.int32, (4, 128), 1)
    table = jnp.zeros((4, 128), jnp.float32)
    for i in range(QR // QB):
        query = placed[step, i * QB : (i + 1) * QB, :].astype(jnp.bfloat16)
        product = lax.dot_general(
            query, key, (((1,), (1,)), ((), ())), preferred_element_type=jnp.float32
        )
        for j in range(KR // QB):
            block = product[:, j * QB : (j + 1) * QB]
            peak = jnp.max(jnp.abs(block), axis=(0, 1), keepdims=True)
            scale = (peak + EPSILON).astype(jnp.bfloat16).astype(jnp.float32)
            values[0, i * QB : (i + 1) * QB, j * QB : (j + 1) * QB] = (
                block * (1.0 / scale)
            ).astype(jnp.bfloat16)
            table = jnp.where((row_at == j) & (col_at == i), scale, table)
    scales[0] = table[:, : QR // QB].astype(jnp.bfloat16)


def absorb(meta, rows, blocks, earlier=None):
    swapped = earlier is not None

    def head(step, meta, rows):
        half = 1 - meta[0] if swapped else meta[0]
        return (half * HALF + step, 0, 0)

    whole = pl.BlockSpec((NX * NZ * NC, 8, WIDE), lambda step, meta, rows: (0, 0, 0))
    anywhere = pl.BlockSpec(memory_space=pl.ANY)
    return pl.pallas_call(
        functools.partial(absorb_kernel, swapped),
        out_shape=(
            jax.ShapeDtypeStruct((H_DEV, QR, KR), jnp.bfloat16),
            jax.ShapeDtypeStruct((H_DEV, KR // QB, QR // QB), jnp.bfloat16),
        ),
        grid_spec=pltpu.PrefetchScalarGridSpec(
            num_scalar_prefetch=2,
            grid=(HALF,),
            in_specs=[whole] * 4 + ([anywhere] * 2 if swapped else []),
            out_specs=(
                pl.BlockSpec((1, QR, KR), head),
                pl.BlockSpec((1, KR // QB, QR // QB), head),
            ),
            scratch_shapes=[pltpu.VMEM((HALF, LAT, DH), jnp.float32)],
        ),
        input_output_aliases={6: 0, 7: 1} if swapped else {},
        compiler_params=pltpu.CompilerParams(vmem_limit_bytes=32 * 2**20),
        cost_estimate=pl.CostEstimate(
            flops=2 * HALF * QR * KR * DH,
            bytes_accessed=HALF * QR * KR * 2 + LAT * WIDE * 2,
            transcendentals=0,
        ),
    )(meta, rows, *blocks, *(earlier or ()))


def gather_phase(block, target):
    return [block] + [lax.ppermute(block, AXES, target(k)) for k in (1, 2, 3)]


def on_device(trainer_rows, route):
    group = lax.axis_index("head")
    replica = lax.axis_index("rep")
    held = trainer_rows[0, 0]
    owners = lax.dynamic_slice(
        route, (group, replica, 0, 0), (1, 1, NZ, 1)
    ).reshape(NZ)
    chosen = owners[None, :] == jnp.arange(NZ, dtype=jnp.int32)[:, None]
    picks = jnp.sum(jnp.where(chosen, jnp.arange(NZ, dtype=jnp.int32)[None], 0), axis=1)
    ordered = held[picks].reshape(NZ, 8, NC, WIDE).transpose(0, 2, 1, 3)
    mine = route[:, :, :, 0] == group
    rows = jnp.sum(jnp.where(mine, route[:, :, :, 1], 0), axis=2)
    meta = jnp.stack([replica % NC, replica // (NY * NC), replica // NC % NY])
    arrived = lax.all_to_all(
        ordered.reshape(NZ * NC, 8, WIDE),
        AXES,
        split_axis=0,
        concat_axis=0,
        axis_index_groups=columns(),
        tiled=True,
    )
    line = jnp.concatenate(gather_phase(arrived, first_axis))
    own = gather_phase(line, second_axis)
    other = [lax.ppermute(b, AXES, other_core()) for b in own]
    earlier = absorb(meta, rows, own)
    values, scales = absorb(meta, rows, other, earlier)
    return values, scales.transpose(0, 2, 1)


def solution(mesh):
    return jax.shard_map(
        on_device,
        mesh=mesh,
        in_specs=(P("head", "rep", None, None, None), P()),
        out_specs=(P("head", None, None), P("head", None, None)),
        check_vma=False,
    )
```

time: 140 us -> 64 us (0.46)
  waiting for transfers between devices: 48.1 us -> 13.2 us
  other arithmetic: 27.8 us -> 1.2 us
  matrix products: 21.5 us -> 0 us
  starting transfers between devices: 0.04 us -> 14.2 us
  Pallas kernels: 0 us -> 13.8 us
  between operations: 14.2 us -> 0.74 us
  local copies, waits for them, and re-layouts: 11.2 us -> 1.65 us
  blocking collectives: 16.7 us -> 18.9 us
    all_gather x1 -> x0, waiting for transfers between devices: 48.1 us -> none  [on_device(): everything = lax.all_gather(arrived, 'rep', axis=0, tiled=True)]
    dot_general x1 -> x0, matrix products: 21.5 us -> none  [absorb(): jnp.einsum('hqd,hkd->hqk', query_heads, key_heads, preferred_element_type...]
    ppermute x0 -> x10, starting transfers between devices: none -> 14.2 us  [the longest x6 8.98 us: gather_phase(): return [block] + [lax.ppermute(block, AXES, target(k)) for k in (1, 2, 3)]]
    convert_element_type x2 -> x0, other arithmetic: 14.1 us -> none  [the longest x1 14.1 us: absorb(): values = (products.reshape(head_count, row_blocks, QB, col_count) / sprea...]
    pallas_call x0 -> x2, Pallas kernels: none -> 13.8 us  [absorb(): pl.pallas_call(functools.partial(absorb_kernel, swapped), out_shape=(jax....]
    ppermute x0 -> x10, waiting for transfers between devices: none -> 13.2 us  [the longest x6 13.2 us: gather_phase(): return [block] + [lax.ppermute(block, AXES, target(k)) for k in (1, 2, 3)]]
    reduce_max x2 -> x0, other arithmetic: 9.99 us -> none  [the longest x1 9.79 us: absorb(): row_peak = jnp.max(banded, axis=2)]
    gather x2 -> x1, local copies, waits for them, and re-layouts: 5.58 us -> 0.56 us  [on_device(): ordered = held[picks].reshape(NZ, 8, NC, WIDE).transpose(0, 2, 1, 3)]
  transfers between devices with their start and end apart: 1 -> 10, of which waited for: 1 -> 5; matrix products, arithmetic and copies ran while one was open for 1% -> 2% of each run, Pallas kernels for 0% -> 12%
where the time goes in v1:
time: 64 us; the launch traced here: 63.8 us
  blocking collectives  18.9 us (30%)
  starting transfers between devices  14.2 us (22%)
  Pallas kernels  13.8 us (22%)
  waiting for transfers between devices  13.2 us (21%)
  local copies, waits for them, and re-layouts  1.65 us (3%)
  other arithmetic  1.2 us (2%)
  between operations  0.74 us (1%)
    all_to_all x1, blocking collectives, on_device(): lax.all_to_all(ordered.reshape(NZ * NC, 8, WIDE), AXES, split_axis=0, con...  18.9 us
    pallas_call x2, Pallas kernels, absorb(): pl.pallas_call(functools.partial(absorb_kernel, swapped), out_shape=(jax....  13.8 us
    ppermute x6, waiting for transfers between devices, gather_phase(): return [block] + [lax.ppermute(block, AXES, target(k)) for k in (1, 2, 3)]  13.2 us
    ppermute x6, starting transfers between devices, gather_phase(): return [block] + [lax.ppermute(block, AXES, target(k)) for k in (1, 2, 3)]  8.98 us
    ppermute x4, starting transfers between devices, on_device(): other = [lax.ppermute(b, AXES, other_core()) for b in own]  5.23 us
  transfers between devices with their start and end apart: 10, of which 5 were waited for; matrix products, arithmetic and copies ran while one was open for 2% of the time, Pallas kernels for 12%

profile of v1, /device:TPU:1, one launch (start us, length us, event | category | flops | bytes accessed | tf_op | source)
XLA Modules:
  0.0 63.8 jit_solution(9964648273015686491)
XLA Ops:
  0.6 0.0 copy-start
  0.6 1.0 %dynamic-slice_reduce_fusion = s32[8]{0:T(128)S(1)} fusion(s32[8,32,8,2]{1,3,2,0:T(2,128)} %param.3, s32[]{:T(128)S(6)} %select_n.48, s32[]{:T(128)S(6)} %select_n.49), kind=kLoop, calls=%fused_computation.11 | loop fusion | bytes 72 | tf_op jit(solution)/shard_map/dynamic_slice | solution.py:150
  1.7 0.1 select_reduce_fusion
  1.8 0.6 gather_fusion
  2.4 18.9 %all_to_all.5 = bf16[16,8,512]{2,1,0:T(8,128)(2,1)S(1)} all-to-all(bf16[16,8,512]{2,1,0:T(8,128)(2,1)S(1)} %bitcast.11), channel_id=1, replica_groups={{0,1,32,33,64,65,96,97,128,129,160,161,192,193,224,225},{2,3,34,35,66,6..., dimensions={0} | all-to-all | bytes 262144 | tf_op jit(solution)/shard_map/all_to_all | solution.py:159
  21.4 2.7 %collective-permute-start = (bf16[16,8,512]{2,1,0:T(8,128)(2,1)S(1)}, bf16[16,8,512]{2,1,0:T(8,128)(2,1)S(1)}, u32[]{:S(2)}, u32[]{:S(2)}) collective-permute-start(bf16[16,8,512]{2,1,0:T(8,128)(2,1)S(1)} %all_to_all.5), channel_id=1, source_target_pairs={{0,24},{1,7},{2,26},{3,1},{4,28},{5,3},{6,30},{7,5},{8,0},{9,15},{... | collective-permute-start | bytes 393224 | tf_op jit(solution)/shard_map/ppermute | solution.py:143
  24.1 1.6 %collective-permute-start.1 = (bf16[16,8,512]{2,1,0:T(8,128)(2,1)S(1)}, bf16[16,8,512]{2,1,0:T(8,128)(2,1)S(1)}, u32[]{:S(2)}, u32[]{:S(2)}) collective-permute-start(bf16[16,8,512]{2,1,0:T(8,128)(2,1)S(1)} %all_to_all.5), channel_id=1, source_target_pairs={{0,16},{1,5},{2,18},{3,7},{4,20},{5,1},{6,22},{7,3},{8,24},{9,13},... | collective-permute-start | bytes 393224 | tf_op jit(solution)/shard_map/ppermute | solution.py:143
  25.8 0.3 collective-permute-done
  26.1 3.8 %collective-permute-done.1 = bf16[16,8,512]{2,1,0:T(8,128)(2,1)S(1)} collective-permute-done((bf16[16,8,512]{2,1,0:T(8,128)(2,1)S(1)}, bf16[16,8,512]{2,1,0:T(8,128)(2,1)S(1)}, u32[]{:S(2)}, u32[]{:S(2)}) %collective-permute-start.1) | collective-permute-done | bytes 131104 | tf_op jit(solution)/shard_map/ppermute | solution.py:143
  29.9 1.0 %collective-permute-done.2 = bf16[16,8,512]{2,1,0:T(8,128)(2,1)S(1)} collective-permute-done((bf16[16,8,512]{2,1,0:T(8,128)(2,1)S(1)}, bf16[16,8,512]{2,1,0:T(8,128)(2,1)S(1)}, u32[]{:S(2)}, u32[]{:S(2)}) %collective-permute-start.2) | collective-permute-done | bytes 131104 | tf_op jit(solution)/shard_map/ppermute | solution.py:143
  30.9 1.0 %collective-permute-start.8 = (bf16[64,8,512]{2,1,0:T(8,128)(2,1)S(1)}, bf16[64,8,512]{2,1,0:T(8,128)(2,1)S(1)}, u32[]{:S(2)}, u32[]{:S(2)}) collective-permute-start(bf16[64,8,512]{2,1,0:T(8,128)(2,1)S(1)} %constant_dynamic-update-slice_fusion.b0), channel_id=1, source_target_pairs={{0,2},{1,9},{2,4},{3,11},{4,6},{5,13},{6,0},{7,15},{8,10},{9,17},{... | collective-permute-start | bytes 1572872 | tf_op jit(solution)/shard_map/ppermute | solution.py:143
  31.9 2.5 %collective-permute-start.6 = (bf16[64,8,512]{2,1,0:T(8,128)(2,1)S(1)}, bf16[64,8,512]{2,1,0:T(8,128)(2,1)}, u32[]{:S(2)}, u32[]{:S(2)}) collective-permute-start(bf16[64,8,512]{2,1,0:T(8,128)(2,1)S(1)} %constant_dynamic-update-slice_fusion.b0), channel_id=1, source_target_pairs={{0,4},{1,17},{2,6},{3,19},{4,0},{5,21},{6,2},{7,23},{8,12},{9,25},... | collective-permute-start | bytes 1572872 | tf_op jit(solution)/shard_map/ppermute | solution.py:143
  34.3 1.2 %collective-permute-start.4 = (bf16[64,8,512]{2,1,0:T(8,128)(2,1)S(1)}, bf16[64,8,512]{2,1,0:T(8,128)(2,1)}, u32[]{:S(2)}, u32[]{:S(2)}) collective-permute-start(bf16[64,8,512]{2,1,0:T(8,128)(2,1)S(1)} %constant_dynamic-update-slice_fusion.b0), channel_id=1, source_target_pairs={{0,6},{1,25},{2,0},{3,27},{4,2},{5,29},{6,4},{7,31},{8,14},{9,1},{... | collective-permute-start | bytes 1572872 | tf_op jit(solution)/shard_map/ppermute | solution.py:143
  35.5 1.9 %collective-permute-start.3 = (bf16[64,8,512]{2,1,0:T(8,128)(2,1)S(1)}, bf16[64,8,512]{2,1,0:T(8,128)(2,1)S(1)}, u32[]{:S(2)}, u32[]{:S(2)}) collective-permute-start(bf16[64,8,512]{2,1,0:T(8,128)(2,1)S(1)} %constant_dynamic-update-slice_fusion.b0), channel_id=1, source_target_pairs={{0,1},{1,0},{2,3},{3,2},{4,5},{5,4},{6,7},{7,6},{8,9},{9,8},{10,11... | collective-permute-start | bytes 1572872 | tf_op jit(solution)/shard_map/ppermute | solution.py:169
  37.3 3.2 %collective-permute-done.8.b3 = bf16[64,8,512]{2,1,0:T(8,128)(2,1)S(1)} collective-permute-done((bf16[64,8,512]{2,1,0:T(8,128)(2,1)S(1)}, bf16[64,8,512]{2,1,0:T(8,128)(2,1)S(1)}, u32[]{:S(2)}, u32[]{:S(2)}) %collective-permute-start.8) | collective-permute-done | bytes 524320 | tf_op jit(solution)/shard_map/ppermute | solution.py:143
  40.5 1.4 %collective-permute-start.9 = (bf16[64,8,512]{2,1,0:T(8,128)(2,1)S(1)}, bf16[64,8,512]{2,1,0:T(8,128)(2,1)S(1)}, u32[]{:S(2)}, u32[]{:S(2)}) collective-permute-start(bf16[64,8,512]{2,1,0:T(8,128)(2,1)S(1)} %collective-permute-done.8.b3), channel_id=1, source_target_pairs={{0,1},{1,0},{2,3},{3,2},{4,5},{5,4},{6,7},{7,6},{8,9},{9,8},{10,11... | collective-permute-start | bytes 1572872 | tf_op jit(solution)/shard_map/ppermute | solution.py:169
  41.9 5.0 %collective-permute-done.6.b2 = bf16[64,8,512]{2,1,0:T(8,128)(2,1)} collective-permute-done((bf16[64,8,512]{2,1,0:T(8,128)(2,1)S(1)}, bf16[64,8,512]{2,1,0:T(8,128)(2,1)}, u32[]{:S(2)}, u32[]{:S(2)}) %collective-permute-start.6) | collective-permute-done | bytes 524320 | tf_op jit(solution)/shard_map/ppermute | solution.py:143
  46.9 2.0 %collective-permute-start.7 = (bf16[64,8,512]{2,1,0:T(8,128)(2,1)}, bf16[64,8,512]{2,1,0:T(8,128)(2,1)S(1)}, u32[]{:S(2)}, u32[]{:S(2)}) collective-permute-start(bf16[64,8,512]{2,1,0:T(8,128)(2,1)} %collective-permute-done.6.b2), channel_id=1, source_target_pairs={{0,1},{1,0},{2,3},{3,2},{4,5},{5,4},{6,7},{7,6},{8,9},{9,8},{10,11... | collective-permute-start | bytes 1572872 | tf_op jit(solution)/shard_map/ppermute | solution.py:169
  48.9 0.0 collective-permute-done.4.b1
  48.9 0.0 collective-permute-start.5
  48.9 0.1 pad_add_fusion.meta
  48.9 1.0 %fusion.rows = s32[8,32]{1,0:T(8,128)S(1)} fusion(s32[8,32,8,2]{1,3,2,0:T(2,128)} %param.3, s32[]{:T(128)S(6)} %axis_index.25), kind=kLoop, calls=%fused_computation.3 | loop fusion | flops 5888 | bytes 17412 | tf_op jit(solution)/shard_map/reduce_sum | solution.py:157
  49.9 7.5 %shard_map.41 = (bf16[8,1536,512]{2,1,0:T(8,128)(2,1)}, bf16[8,4,12]{2,1,0:T(4,128)(2,1)}) custom-call(s32[3]{0:T(128)S(1)} %pad_add_fusion.meta, s32[8,32]{1,0:T(8,128)S(1)} %fusion.rows, bf16[64,8,512]{2,1,0:T(8,128)(2,1)S(1)} %constant_dynamic-update-slice_fusion.b0, bf16[64,8,512]{2,1,0:T(8,128)(2,1)} %collective-permute-done.4.b1, ...), custom_call_target="tpu_custom_call" | custom-call | flops 805306368 | bytes 8388608 | tf_op jit(solution)/shard_map/pallas_call | solution.py:116
  57.5 6.3 %shard_map.42 = (bf16[8,1536,512]{2,1,0:T(8,128)(2,1)}, bf16[8,4,12]{2,1,0:T(4,128)(2,1)}) custom-call(s32[3]{0:T(128)S(1)} %pad_add_fusion.meta, s32[8,32]{1,0:T(8,128)S(1)} %fusion.rows, bf16[64,8,512]{2,1,0:T(8,128)(2,1)S(1)} %collective-permute-done.3.b0, ...), custom_call_target="tpu_custom_call", output_to_operand_aliasing={{0}: (6, {}), {1}: (7, {})} | custom-call | flops 805306368 | bytes 8388608 | tf_op jit(solution)/shard_map/pallas_call | solution.py:116
  (14 shorter events, 0.1 us)
Async XLA Ops:
  0.6 1.2 %copy-start = (bf16[1,1,8,8,1024]{4,3,2,1,0:T(8,128)(2,1)S(1)}, bf16[1,1,8,8,1024]{4,3,2,1,0:T(8,128)(2,1)}, u32[]{:S(2)}) copy-start(bf16[1,1,8,8,1024]{4,3,2,1,0:T(8,128)(2,1)} %param.2) | copy-start | bytes 393220
  21.4 4.7 %collective-permute-start = (bf16[16,8,512]{2,1,0:T(8,128)(2,1)S(1)}, bf16[16,8,512]{2,1,0:T(8,128)(2,1)S(1)}, u32[]{:S(2)}, u32[]{:S(2)}) collective-permute-start(bf16[16,8,512]{2,1,0:T(8,128)(2,1)S(1)} %all_to_all.5), channel_id=1, source_target_pairs={{0,24},{1,7},{2,26},{3,1},{4,28},{5,3},{6,30},{7,5},{8,0},{9,15},{... | collective-permute-start | bytes 393224 | tf_op jit(solution)/shard_map/ppermute | solution.py:143
  24.1 6.7 %collective-permute-start.2 = (bf16[16,8,512]{2,1,0:T(8,128)(2,1)S(1)}, bf16[16,8,512]{2,1,0:T(8,128)(2,1)S(1)}, u32[]{:S(2)}, u32[]{:S(2)}) collective-permute-start(bf16[16,8,512]{2,1,0:T(8,128)(2,1)S(1)} %all_to_all.5), channel_id=1, source_target_pairs={{0,8},{1,3},{2,10},{3,5},{4,12},{5,7},{6,14},{7,1},{8,16},{9,11},{... | collective-permute-start | bytes 393224 | tf_op jit(solution)/shard_map/ppermute | solution.py:143
  24.1 5.7 %collective-permute-start.1 = (bf16[16,8,512]{2,1,0:T(8,128)(2,1)S(1)}, bf16[16,8,512]{2,1,0:T(8,128)(2,1)S(1)}, u32[]{:S(2)}, u32[]{:S(2)}) collective-permute-start(bf16[16,8,512]{2,1,0:T(8,128)(2,1)S(1)} %all_to_all.5), channel_id=1, source_target_pairs={{0,16},{1,5},{2,18},{3,7},{4,20},{5,1},{6,22},{7,3},{8,24},{9,13},... | collective-permute-start | bytes 393224 | tf_op jit(solution)/shard_map/ppermute | solution.py:143
  30.9 9.6 %collective-permute-start.8 = (bf16[64,8,512]{2,1,0:T(8,128)(2,1)S(1)}, bf16[64,8,512]{2,1,0:T(8,128)(2,1)S(1)}, u32[]{:S(2)}, u32[]{:S(2)}) collective-permute-start(bf16[64,8,512]{2,1,0:T(8,128)(2,1)S(1)} %constant_dynamic-update-slice_fusion.b0), channel_id=1, source_target_pairs={{0,2},{1,9},{2,4},{3,11},{4,6},{5,13},{6,0},{7,15},{8,10},{9,17},{... | collective-permute-start | bytes 1572872 | tf_op jit(solution)/shard_map/ppermute | solution.py:143
  31.9 15.0 %collective-permute-start.6 = (bf16[64,8,512]{2,1,0:T(8,128)(2,1)S(1)}, bf16[64,8,512]{2,1,0:T(8,128)(2,1)}, u32[]{:S(2)}, u32[]{:S(2)}) collective-permute-start(bf16[64,8,512]{2,1,0:T(8,128)(2,1)S(1)} %constant_dynamic-update-slice_fusion.b0), channel_id=1, source_target_pairs={{0,4},{1,17},{2,6},{3,19},{4,0},{5,21},{6,2},{7,23},{8,12},{9,25},... | collective-permute-start | bytes 1572872 | tf_op jit(solution)/shard_map/ppermute | solution.py:143
  34.3 14.5 %collective-permute-start.4 = (bf16[64,8,512]{2,1,0:T(8,128)(2,1)S(1)}, bf16[64,8,512]{2,1,0:T(8,128)(2,1)}, u32[]{:S(2)}, u32[]{:S(2)}) collective-permute-start(bf16[64,8,512]{2,1,0:T(8,128)(2,1)S(1)} %constant_dynamic-update-slice_fusion.b0), channel_id=1, source_target_pairs={{0,6},{1,25},{2,0},{3,27},{4,2},{5,29},{6,4},{7,31},{8,14},{9,1},{... | collective-permute-start | bytes 1572872 | tf_op jit(solution)/shard_map/ppermute | solution.py:143
  35.5 22.0 %collective-permute-start.3 = (bf16[64,8,512]{2,1,0:T(8,128)(2,1)S(1)}, bf16[64,8,512]{2,1,0:T(8,128)(2,1)S(1)}, u32[]{:S(2)}, u32[]{:S(2)}) collective-permute-start(bf16[64,8,512]{2,1,0:T(8,128)(2,1)S(1)} %constant_dynamic-update-slice_fusion.b0), channel_id=1, source_target_pairs={{0,1},{1,0},{2,3},{3,2},{4,5},{5,4},{6,7},{7,6},{8,9},{9,8},{10,11... | collective-permute-start | bytes 1572872 | tf_op jit(solution)/shard_map/ppermute | solution.py:169
  40.5 17.0 %collective-permute-start.9 = (bf16[64,8,512]{2,1,0:T(8,128)(2,1)S(1)}, bf16[64,8,512]{2,1,0:T(8,128)(2,1)S(1)}, u32[]{:S(2)}, u32[]{:S(2)}) collective-permute-start(bf16[64,8,512]{2,1,0:T(8,128)(2,1)S(1)} %collective-permute-done.8.b3), channel_id=1, source_target_pairs={{0,1},{1,0},{2,3},{3,2},{4,5},{5,4},{6,7},{7,6},{8,9},{9,8},{10,11... | collective-permute-start | bytes 1572872 | tf_op jit(solution)/shard_map/ppermute | solution.py:169
  46.9 10.5 %collective-permute-start.7 = (bf16[64,8,512]{2,1,0:T(8,128)(2,1)}, bf16[64,8,512]{2,1,0:T(8,128)(2,1)S(1)}, u32[]{:S(2)}, u32[]{:S(2)}) collective-permute-start(bf16[64,8,512]{2,1,0:T(8,128)(2,1)} %collective-permute-done.6.b2), channel_id=1, source_target_pairs={{0,1},{1,0},{2,3},{3,2},{4,5},{5,4},{6,7},{7,6},{8,9},{9,8},{10,11... | collective-permute-start | bytes 1572872 | tf_op jit(solution)/shard_map/ppermute | solution.py:169
  48.9 8.6 %collective-permute-start.5 = (bf16[64,8,512]{2,1,0:T(8,128)(2,1)}, bf16[64,8,512]{2,1,0:T(8,128)(2,1)S(1)}, u32[]{:S(2)}, u32[]{:S(2)}) collective-permute-start(bf16[64,8,512]{2,1,0:T(8,128)(2,1)} %collective-permute-done.4.b1), channel_id=1, source_target_pairs={{0,1},{1,0},{2,3},{3,2},{4,5},{5,4},{6,7},{7,6},{8,9},{9,8},{10,11... | collective-permute-start | bytes 1572872 | tf_op jit(solution)/shard_map/ppermute | solution.py:169

commit v2 on v1

v2 whole, which is shorter than its diff:
```python
import jax
import jax.numpy as jnp
from jax import lax
from jax.experimental import pallas as pl
from jax.experimental.pallas import tpu as pltpu
from jax.sharding import PartitionSpec as P

QR = 1536
KR = 512
DH = 128
H_DEV = 8
QB = 128
LAT = QR + KR
NZ = 8
NX = 4
NY = 4
NC = 2
STEPS = NZ // NC
Q_BLOCKS = QR // QB
K_BLOCKS = KR // QB
SEND = 4
HALF = H_DEV // 2
WIDE = HALF * DH
EPSILON = 1e-06
AXES = ("head", "rep")


def index_of(z, x, y, c):
    return (z % NZ) * (NX * NY * NC) + (x % NX) * (NY * NC) + (y % NY) * NC + c


def pairs(target):
    every = [
        (z, x, y, c)
        for z in range(NZ)
        for x in range(NX)
        for y in range(NY)
        for c in range(NC)
    ]
    return [(index_of(*d), index_of(*target(*d))) for d in every]


def z_shift(core, step):
    if core == 0:
        return step
    return -step if step else NZ // 2


def along_z(step):
    return pairs(lambda z, x, y, c: (z + z_shift(c, step), x, y, c))


def first_axis(k):
    return pairs(lambda z, x, y, c: (z, x - k, y, c) if c == 0 else (z, x, y - k, c))


def second_axis(k):
    return pairs(lambda z, x, y, c: (z, x, y - k, c) if c == 0 else (z, x - k, y, c))


def other_core():
    return pairs(lambda z, x, y, c: (z, x, y, 1 - c))


def choose(blocks, owners, messages, place):
    group = lax.axis_index("head")
    core = lax.axis_index("rep") & (NC - 1)
    wide = [blocks[s].astype(jnp.float32) for s in range(NZ)]
    for step, message in enumerate(messages):
        shift = jnp.where(core == 0, z_shift(0, step), z_shift(1, step))
        wanted = (group + shift) & (NZ - 1)
        block = wide[0]
        for s in range(1, NZ):
            block = jnp.where(owners[s : s + 1] == wanted, wide[s], block)
        message[place] = block.astype(jnp.bfloat16)


def prepare_kernel(route, held, *refs):
    messages, rows, other_owners = refs[:STEPS], refs[-2], refs[-1]
    group = lax.axis_index("head")
    replica = lax.axis_index("rep")
    rows[...] = jnp.sum(
        jnp.where(route[:, :, 0, :] == group, route[:, :, 1, :], 0), axis=1
    )
    slots = route[group][:, 0, :]
    lanes = lax.broadcasted_iota(jnp.int32, slots.shape, 1)
    owners = [
        jnp.sum(jnp.where(lanes == source, slots, 0), axis=1, keepdims=True)
        for source in (replica, replica ^ 1)
    ]
    other_owners[...] = jnp.broadcast_to(owners[1], other_owners.shape)
    choose(held, owners[0], messages, 0)


def complete_kernel(swapped, owners, *refs):
    choose(swapped, owners[:, :1], refs[STEPS:], 1)


def prepare(held, route):
    vector = pl.BlockSpec(memory_space=pltpu.VMEM)
    params = pltpu.CompilerParams(vmem_limit_bytes=16 * 2**20)
    message = jax.ShapeDtypeStruct((NC, *held.shape[1:]), held.dtype)
    swapped = move(held, other_core())
    *messages, rows, owners = pl.pallas_call(
        prepare_kernel,
        out_shape=[message] * STEPS
        + [
            jax.ShapeDtypeStruct((NZ, NX * NY * NC), jnp.int32),
            jax.ShapeDtypeStruct((NZ, 128), jnp.int32),
        ],
        in_specs=[vector] * 2,
        out_specs=[vector] * (STEPS + 2),
        compiler_params=params,
    )(route.transpose(0, 2, 3, 1), held)
    messages = pl.pallas_call(
        complete_kernel,
        out_shape=[message] * STEPS,
        in_specs=[vector] * (STEPS + 2),
        out_specs=[vector] * STEPS,
        input_output_aliases={2 + step: step for step in range(STEPS)},
        compiler_params=params,
    )(swapped, owners, *messages)
    return messages, rows


def absorb_kernel(*refs):
    far_rows, own_line, other_line = refs[:3]
    own = refs[3:6]
    other = refs[6:9]
    values, scales, rows, placed, scaled, tables, sems, scale_sem, row_sem = refs[9:]
    at_z = lax.axis_index("head")
    replica = lax.axis_index("rep")
    core = replica & (NC - 1)
    at_x = replica // (NY * NC)
    at_y = (replica // NC) & (NY - 1)
    fetch = pltpu.make_async_copy(far_rows, rows, row_sem)
    fetch.start()
    fetch.wait()
    for arrays, holder in (((own_line, *own), core), ((other_line, *other), 1 - core)):
        planes = []
        for step in range(STEPS):
            ahead = step if step else NZ // 2
            planes.append((at_z + jnp.where(holder == 0, NZ - step, ahead)) & (NZ - 1))
        for second in range(NX):

            def body(first, carry, second=second, planes=planes):
                x = (at_x + jnp.where(holder == 0, first, second)) & (NX - 1)
                y = (at_y + jnp.where(holder == 0, second, first)) & (NY - 1)
                at = x * (NY * NC) + y * NC
                for step in range(STEPS):
                    for i in range(NC):
                        row = pl.multiple_of(rows[planes[step], at + (holder ^ i)], 8)
                        index = first * (STEPS * NC) + step * NC + i
                        block = arrays[second][index].astype(jnp.float32)
                        for h in range(H_DEV):
                            placed[h, pl.ds(row, 8), :] = block[:, h * DH : (h + 1) * DH]
                return carry

            lax.fori_loop(0, NX, body, 0)

    def writes(h, k):
        at = pl.ds(k * SEND * QB, SEND * QB)
        return pltpu.make_async_copy(scaled.at[h, at], values.at[h, at], sems.at[h, k])

    row_at = lax.broadcasted_iota(jnp.int32, (K_BLOCKS, 128), 0)
    col_at = lax.broadcasted_iota(jnp.int32, (K_BLOCKS, 128), 1)
    for h in range(H_DEV):
        key = placed[h, QR:, :].astype(jnp.bfloat16)
        table = jnp.zeros((K_BLOCKS, 128), jnp.float32)
        for i in range(Q_BLOCKS):
            query = placed[h, i * QB : (i + 1) * QB, :].astype(jnp.bfloat16)
            product = lax.dot_general(
                query, key, (((1,), (1,)), ((), ())), preferred_element_type=jnp.float32
            )
            peaks = jnp.max(jnp.abs(product), axis=0, keepdims=True)
            for j in range(K_BLOCKS):
                cols = slice(j * QB, (j + 1) * QB)
                peak = jnp.max(peaks[:, cols], axis=1, keepdims=True)
                scale = (peak + EPSILON).astype(jnp.bfloat16).astype(jnp.float32)
                scaled[h, i * QB : (i + 1) * QB, cols] = (
                    product[:, cols] * (1.0 / scale)
                ).astype(jnp.bfloat16)
                table = jnp.where((row_at == j) & (col_at == i), scale, table)
            if (i + 1) % SEND == 0:
                writes(h, i // SEND).start()
        tables[h] = table[:, :Q_BLOCKS].astype(jnp.bfloat16)
    finish = pltpu.make_async_copy(tables, scales, scale_sem)
    finish.start()
    for h in range(H_DEV):
        for k in range(Q_BLOCKS // SEND):
            writes(h, k).wait()
    finish.wait()


def absorb(rows, own_line, other_line, own, other):
    vector = pl.BlockSpec(memory_space=pltpu.VMEM)
    anywhere = pl.BlockSpec(memory_space=pl.ANY)
    return pl.pallas_call(
        absorb_kernel,
        out_shape=(
            jax.ShapeDtypeStruct((H_DEV, QR, KR), jnp.bfloat16),
            jax.ShapeDtypeStruct((H_DEV, K_BLOCKS, Q_BLOCKS), jnp.bfloat16),
        ),
        in_specs=[vector] * (3 + len(own) + len(other)),
        out_specs=(anywhere, anywhere),
        scratch_shapes=[
            pltpu.SMEM(rows.shape, rows.dtype),
            pltpu.VMEM((H_DEV, LAT, DH), jnp.float32),
            pltpu.VMEM((H_DEV, QR, KR), jnp.bfloat16),
            pltpu.VMEM((H_DEV, K_BLOCKS, Q_BLOCKS), jnp.bfloat16),
            pltpu.SemaphoreType.DMA((H_DEV, Q_BLOCKS // SEND)),
            pltpu.SemaphoreType.DMA,
            pltpu.SemaphoreType.DMA,
        ],
        compiler_params=pltpu.CompilerParams(vmem_limit_bytes=32 * 2**20),
        cost_estimate=pl.CostEstimate(
            flops=2 * H_DEV * QR * KR * DH,
            bytes_accessed=H_DEV * QR * KR * 2,
            transcendentals=0,
        ),
    )(rows, own_line, other_line, *own, *other)


def move(block, target):
    return lax.ppermute(block, AXES, target)


def gather_phase(block, target):
    return [block] + [lax.ppermute(block, AXES, target(k)) for k in (1, 2, 3)]


def on_device(trainer_rows, route):
    messages, rows = prepare(trainer_rows[0, 0], route)
    arrived = jnp.concatenate(
        [lax.ppermute(m, AXES, along_z(s)) for s, m in enumerate(messages)]
    )
    line = jnp.concatenate(gather_phase(arrived, first_axis))
    own = [move(line, second_axis(k)) for k in (1, 2, 3)]
    other = [move(piece, other_core()) for piece in own]
    other_line = move(line, other_core())
    values, scales = absorb(rows, line, other_line, own, other)
    return values, scales.transpose(0, 2, 1)


def solution(mesh):
    return jax.shard_map(
        on_device,
        mesh=mesh,
        in_specs=(P("head", "rep", None, None, None), P()),
        out_specs=(P("head", None, None), P("head", None, None)),
        check_vma=False,
    )
```

time: 64 us -> 55.4 us (0.87)
  blocking collectives: 18.9 us -> 0 us
  starting transfers between devices: 14.2 us -> 25.4 us
  Pallas kernels: 13.8 us -> 7.6 us
  waiting for transfers between devices: 13.2 us -> 19.3 us
  other arithmetic: 1.2 us -> 0 us
    all_to_all x1 -> x0, blocking collectives: 18.9 us -> none  [on_device(): lax.all_to_all(ordered.reshape(NZ * NC, 8, WIDE), AXES, split_axis=0, con...]
    ppermute x4 -> x12, starting transfers between devices: 5.23 us -> 21.7 us  [the longest x4 11.9 us: on_device(): lax.ppermute(m, AXES, along_z(s))]
    ppermute x4 -> x12, waiting for transfers between devices: 0.01 us -> 13.6 us  [the longest x8 12.7 us: move(): return lax.ppermute(block, AXES, target)]
    ppermute x6 -> x3, waiting for transfers between devices: 13.2 us -> 5.66 us  [gather_phase(): return [block] + [lax.ppermute(block, AXES, target(k)) for k in (1, 2, 3)]]
    pallas_call x2 -> x3, Pallas kernels: 13.8 us -> 7.6 us  [the longest x1 7.36 us: absorb(): pl.pallas_call(absorb_kernel, out_shape=(jax.ShapeDtypeStruct((H_DEV, QR,...]
    ppermute x6 -> x3, starting transfers between devices: 8.98 us -> 3.77 us  [gather_phase(): return [block] + [lax.ppermute(block, AXES, target(k)) for k in (1, 2, 3)]]
    unnamed x5 -> x9, local copies, waits for them, and re-layouts: 0.04 us -> 1.78 us
    reduce_sum x2 -> x0, other arithmetic: 1.1 us -> none  [the longest x1 0.99 us: on_device(): rows = jnp.sum(jnp.where(mine, route[:, :, :, 1], 0), axis=2)]
  transfers between devices with their start and end apart: 10 -> 15, of which waited for: 5 -> 8; matrix products, arithmetic and copies ran while one was open for 2% -> 0% of each run, Pallas kernels for 12% -> 0%
where the time goes in v2:
time: 55.4 us; the launch traced here: 55 us
  starting transfers between devices  25.4 us (46%)
  waiting for transfers between devices  19.3 us (35%)
  Pallas kernels  7.6 us (14%)
  local copies, waits for them, and re-layouts  1.8 us (3%)
  between operations  0.9 us (2%)
    ppermute x8, waiting for transfers between devices, move(): return lax.ppermute(block, AXES, target)  12.7 us
    ppermute x4, starting transfers between devices, on_device(): lax.ppermute(m, AXES, along_z(s))  11.9 us
    ppermute x8, starting transfers between devices, move(): return lax.ppermute(block, AXES, target)  9.76 us
    pallas_call x1, Pallas kernels, absorb(): pl.pallas_call(absorb_kernel, out_shape=(jax.ShapeDtypeStruct((H_DEV, QR,...  7.36 us
    ppermute x3, waiting for transfers between devices, gather_phase(): return [block] + [lax.ppermute(block, AXES, target(k)) for k in (1, 2, 3)]  5.66 us
    ppermute x3, starting transfers between devices, gather_phase(): return [block] + [lax.ppermute(block, AXES, target(k)) for k in (1, 2, 3)]  3.77 us
    unnamed x9, local copies, waits for them, and re-layouts  1.78 us
  transfers between devices with their start and end apart: 15, of which 8 were waited for; matrix products, arithmetic and copies ran while one was open for 0% of the time, Pallas kernels for 0%

profile of v2, /device:TPU:1, one launch (start us, length us, event | category | flops | bytes accessed | tf_op | source)
XLA Modules:
  0.0 55.0 jit_solution(2111561058672015529)
XLA Ops:
  0.6 3.3 %collective-permute-start = (bf16[8,8,1024]{2,1,0:T(8,128)(2,1)}, bf16[8,8,1024]{2,1,0:T(8,128)(2,1)S(1)}, u32[]{:S(2)}, u32[]{:S(2)}) collective-permute-start(bf16[8,8,1024]{2,1,0:T(8,128)(2,1)} %bitcast.3), channel_id=1, source_target_pairs={{0,1},{1,0},{2,3},{3,2},{4,5},{5,4},{6,7},{7,6},{8,9},{9,8},{10,11... | collective-permute-start | bytes 393224 | tf_op jit(solution)/shard_map/ppermute | solution.py:225
  4.0 0.9 %copy-done = bf16[1,1,8,8,1024]{4,3,2,1,0:T(8,128)(2,1)S(1)} copy-done((bf16[1,1,8,8,1024]{4,3,2,1,0:T(8,128)(2,1)S(1)}, bf16[1,1,8,8,1024]{4,3,2,1,0:T(8,128)(2,1)}, u32[]{:S(2)}) %copy-start) | copy-done | bytes 131096
  4.9 0.8 %copy-done.1 = s32[8,32,8,2]{1,3,2,0:T(2,128)S(1)} copy-done((s32[8,32,8,2]{1,3,2,0:T(2,128)S(1)}, s32[8,32,8,2]{1,3,2,0:T(2,128)}, u32[]{:S(2)}) %copy-start.1) | copy-done | bytes 16408
  5.7 0.1 shard_map.41
  6.0 7.1 %collective-permute-start.1 = (bf16[2,8,1024]{2,1,0:T(8,128)(2,1)S(1)}, bf16[2,8,1024]{2,1,0:T(8,128)(2,1)S(1)}, u32[]{:S(2)}, u32[]{:S(2)}) collective-permute-start(bf16[2,8,1024]{2,1,0:T(8,128)(2,1)S(1)} %get-tuple-element.20), channel_id=1, source_target_pairs={{0,0},{1,129},{2,2},{3,131},{4,4},{5,133},{6,6},{7,135},{8,8},{9,1... | collective-permute-start | bytes 98312 | tf_op jit(solution)/shard_map/ppermute | solution.py:235
  13.2 4.7 %collective-permute-start.4 = (bf16[2,8,1024]{2,1,0:T(8,128)(2,1)S(1)}, bf16[2,8,1024]{2,1,0:T(8,128)(2,1)S(1)}, u32[]{:S(2)}, u32[]{:S(2)}) collective-permute-start(bf16[2,8,1024]{2,1,0:T(8,128)(2,1)S(1)} %get-tuple-element.23), channel_id=1, source_target_pairs={{0,96},{1,161},{2,98},{3,163},{4,100},{5,165},{6,102},{7,167},{8,1... | collective-permute-start | bytes 98312 | tf_op jit(solution)/shard_map/ppermute | solution.py:235
  18.0 1.0 %collective-permute-done.4 = bf16[2,8,1024]{2,1,0:T(8,128)(2,1)S(1)} collective-permute-done((bf16[2,8,1024]{2,1,0:T(8,128)(2,1)S(1)}, bf16[2,8,1024]{2,1,0:T(8,128)(2,1)S(1)}, u32[]{:S(2)}, u32[]{:S(2)}) %collective-permute-start.4) | collective-permute-done | bytes 32800 | tf_op jit(solution)/shard_map/ppermute | solution.py:235
  18.9 2.7 %collective-permute-start.5 = (bf16[8,8,1024]{2,1,0:T(8,128)(2,1)S(1)}, bf16[8,8,1024]{2,1,0:T(8,128)(2,1)S(1)}, u32[]{:S(2)}, u32[]{:S(2)}) collective-permute-start(bf16[8,8,1024]{2,1,0:T(8,128)(2,1)S(1)} %get-tuple-element.26), channel_id=1, source_target_pairs={{0,24},{1,7},{2,26},{3,1},{4,28},{5,3},{6,30},{7,5},{8,0},{9,15},{... | collective-permute-start | bytes 393224 | tf_op jit(solution)/shard_map/ppermute | solution.py:229
  21.7 0.3 collective-permute-start.6
  22.0 0.7 %collective-permute-start.7 = (bf16[8,8,1024]{2,1,0:T(8,128)(2,1)S(1)}, bf16[8,8,1024]{2,1,0:T(8,128)(2,1)S(1)}, u32[]{:S(2)}, u32[]{:S(2)}) collective-permute-start(bf16[8,8,1024]{2,1,0:T(8,128)(2,1)S(1)} %get-tuple-element.26), channel_id=1, source_target_pairs={{0,8},{1,3},{2,10},{3,5},{4,12},{5,7},{6,14},{7,1},{8,16},{9,11},{... | collective-permute-start | bytes 393224 | tf_op jit(solution)/shard_map/ppermute | solution.py:229
  22.7 2.3 %collective-permute-done.5 = bf16[8,8,1024]{2,1,0:T(8,128)(2,1)S(1)} collective-permute-done((bf16[8,8,1024]{2,1,0:T(8,128)(2,1)S(1)}, bf16[8,8,1024]{2,1,0:T(8,128)(2,1)S(1)}, u32[]{:S(2)}, u32[]{:S(2)}) %collective-permute-start.5) | collective-permute-done | bytes 131104 | tf_op jit(solution)/shard_map/ppermute | solution.py:229
  25.0 2.1 %collective-permute-done.6 = bf16[8,8,1024]{2,1,0:T(8,128)(2,1)S(1)} collective-permute-done((bf16[8,8,1024]{2,1,0:T(8,128)(2,1)S(1)}, bf16[8,8,1024]{2,1,0:T(8,128)(2,1)S(1)}, u32[]{:S(2)}, u32[]{:S(2)}) %collective-permute-start.6) | collective-permute-done | bytes 131104 | tf_op jit(solution)/shard_map/ppermute | solution.py:229
  27.1 1.3 %collective-permute-done.7 = bf16[8,8,1024]{2,1,0:T(8,128)(2,1)S(1)} collective-permute-done((bf16[8,8,1024]{2,1,0:T(8,128)(2,1)S(1)}, bf16[8,8,1024]{2,1,0:T(8,128)(2,1)S(1)}, u32[]{:S(2)}, u32[]{:S(2)}) %collective-permute-start.7) | collective-permute-done | bytes 131104 | tf_op jit(solution)/shard_map/ppermute | solution.py:229
  28.4 1.3 %collective-permute-start.11 = (bf16[32,8,1024]{2,1,0:T(8,128)(2,1)S(1)}, bf16[32,8,1024]{2,1,0:T(8,128)(2,1)S(1)}, u32[]{:S(2)}, u32[]{:S(2)}) collective-permute-start(bf16[32,8,1024]{2,1,0:T(8,128)(2,1)S(1)} %constant_dynamic-update-slice_fusion.4.refs_1_), channel_id=1, source_target_pairs={{0,2},{1,9},{2,4},{3,11},{4,6},{5,13},{6,0},{7,15},{8,10},{9,17},{... | collective-permute-start | bytes 1572872 | tf_op jit(solution)/shard_map/ppermute | solution.py:225
  29.7 2.5 %collective-permute-start.10 = (bf16[32,8,1024]{2,1,0:T(8,128)(2,1)S(1)}, bf16[32,8,1024]{2,1,0:T(8,128)(2,1)S(1)}, u32[]{:S(2)}, u32[]{:S(2)}) collective-permute-start(bf16[32,8,1024]{2,1,0:T(8,128)(2,1)S(1)} %constant_dynamic-update-slice_fusion.4.refs_1_), channel_id=1, source_target_pairs={{0,4},{1,17},{2,6},{3,19},{4,0},{5,21},{6,2},{7,23},{8,12},{9,25},... | collective-permute-start | bytes 1572872 | tf_op jit(solution)/shard_map/ppermute | solution.py:225
  32.1 1.2 %collective-permute-start.9 = (bf16[32,8,1024]{2,1,0:T(8,128)(2,1)S(1)}, bf16[32,8,1024]{2,1,0:T(8,128)(2,1)S(1)}, u32[]{:S(2)}, u32[]{:S(2)}) collective-permute-start(bf16[32,8,1024]{2,1,0:T(8,128)(2,1)S(1)} %constant_dynamic-update-slice_fusion.4.refs_1_), channel_id=1, source_target_pairs={{0,6},{1,25},{2,0},{3,27},{4,2},{5,29},{6,4},{7,31},{8,14},{9,1},{... | collective-permute-start | bytes 1572872 | tf_op jit(solution)/shard_map/ppermute | solution.py:225
  33.3 0.5 collective-permute-start.8
  33.8 4.2 %collective-permute-done.11.refs_5_ = bf16[32,8,1024]{2,1,0:T(8,128)(2,1)S(1)} collective-permute-done((bf16[32,8,1024]{2,1,0:T(8,128)(2,1)S(1)}, bf16[32,8,1024]{2,1,0:T(8,128)(2,1)S(1)}, u32[]{:S(2)}, u32[]{:S(2)}) %collective-permute-start.11) | collective-permute-done | bytes 524320 | tf_op jit(solution)/shard_map/ppermute | solution.py:225
  38.0 0.4 collective-permute-start.14
  38.4 6.2 %collective-permute-done.10.refs_4_ = bf16[32,8,1024]{2,1,0:T(8,128)(2,1)S(1)} collective-permute-done((bf16[32,8,1024]{2,1,0:T(8,128)(2,1)S(1)}, bf16[32,8,1024]{2,1,0:T(8,128)(2,1)S(1)}, u32[]{:S(2)}, u32[]{:S(2)}) %collective-permute-start.10) | collective-permute-done | bytes 524320 | tf_op jit(solution)/shard_map/ppermute | solution.py:225
  44.6 0.6 %collective-permute-start.13 = (bf16[32,8,1024]{2,1,0:T(8,128)(2,1)S(1)}, bf16[32,8,1024]{2,1,0:T(8,128)(2,1)S(1)}, u32[]{:S(2)}, u32[]{:S(2)}) collective-permute-start(bf16[32,8,1024]{2,1,0:T(8,128)(2,1)S(1)} %collective-permute-done.10.refs_4_), channel_id=1, source_target_pairs={{0,1},{1,0},{2,3},{3,2},{4,5},{5,4},{6,7},{7,6},{8,9},{9,8},{10,11... | collective-permute-start | bytes 1572872 | tf_op jit(solution)/shard_map/ppermute | solution.py:225
  45.3 1.5 %collective-permute-done.13.refs_7_ = bf16[32,8,1024]{2,1,0:T(8,128)(2,1)S(1)} collective-permute-done((bf16[32,8,1024]{2,1,0:T(8,128)(2,1)S(1)}, bf16[32,8,1024]{2,1,0:T(8,128)(2,1)S(1)}, u32[]{:S(2)}, u32[]{:S(2)}) %collective-permute-start.13) | collective-permute-done | bytes 524320 | tf_op jit(solution)/shard_map/ppermute | solution.py:225
  46.8 0.7 %collective-permute-done.12.refs_6_ = bf16[32,8,1024]{2,1,0:T(8,128)(2,1)S(1)} collective-permute-done((bf16[32,8,1024]{2,1,0:T(8,128)(2,1)S(1)}, bf16[32,8,1024]{2,1,0:T(8,128)(2,1)S(1)}, u32[]{:S(2)}, u32[]{:S(2)}) %collective-permute-start.12) | collective-permute-done | bytes 524320 | tf_op jit(solution)/shard_map/ppermute | solution.py:225
  47.5 7.4 %shard_map.43 = (bf16[8,1536,512]{2,1,0:T(8,128)(2,1)}, bf16[8,4,12]{2,1,0:T(4,128)(2,1)}) custom-call(s32[8,32]{1,0:T(8,128)S(1)} %get-tuple-element.14.refs_0_, bf16[32,8,1024]{2,1,0:T(8,128)(2,1)S(1)} %constant_dynamic-update-slice_fusion.4.refs_1_, bf16[32,8,1024]{2,1,0:T(8,128)(2,1)S(1)} %collective-permute-done.8.refs_2_, ...), custom_call_target="tpu_custom_call" | custom-call | flops 1610612736 | bytes 12582912 | tf_op jit(solution)/shard_map/pallas_call | solution.py:198
  (20 shorter events, 0.3 us)
Async XLA Ops:
  0.6 5.2 %collective-permute-start = (bf16[8,8,1024]{2,1,0:T(8,128)(2,1)}, bf16[8,8,1024]{2,1,0:T(8,128)(2,1)S(1)}, u32[]{:S(2)}, u32[]{:S(2)}) collective-permute-start(bf16[8,8,1024]{2,1,0:T(8,128)(2,1)} %bitcast.3), channel_id=1, source_target_pairs={{0,1},{1,0},{2,3},{3,2},{4,5},{5,4},{6,7},{7,6},{8,9},{9,8},{10,11... | collective-permute-start | bytes 393224 | tf_op jit(solution)/shard_map/ppermute | solution.py:225
  4.0 0.9 %copy-start = (bf16[1,1,8,8,1024]{4,3,2,1,0:T(8,128)(2,1)S(1)}, bf16[1,1,8,8,1024]{4,3,2,1,0:T(8,128)(2,1)}, u32[]{:S(2)}) copy-start(bf16[1,1,8,8,1024]{4,3,2,1,0:T(8,128)(2,1)} %param.2) | copy-start | bytes 393220
  4.9 0.8 %copy-start.1 = (s32[8,32,8,2]{1,3,2,0:T(2,128)S(1)}, s32[8,32,8,2]{1,3,2,0:T(2,128)}, u32[]{:S(2)}) copy-start(s32[8,32,8,2]{1,3,2,0:T(2,128)} %param.3) | copy-start | bytes 49156
  6.0 11.9 %collective-permute-start.1 = (bf16[2,8,1024]{2,1,0:T(8,128)(2,1)S(1)}, bf16[2,8,1024]{2,1,0:T(8,128)(2,1)S(1)}, u32[]{:S(2)}, u32[]{:S(2)}) collective-permute-start(bf16[2,8,1024]{2,1,0:T(8,128)(2,1)S(1)} %get-tuple-element.20), channel_id=1, source_target_pairs={{0,0},{1,129},{2,2},{3,131},{4,4},{5,133},{6,6},{7,135},{8,8},{9,1... | collective-permute-start | bytes 98312 | tf_op jit(solution)/shard_map/ppermute | solution.py:235
  13.0 4.9 %collective-permute-start.2 = (bf16[2,8,1024]{2,1,0:T(8,128)(2,1)S(1)}, bf16[2,8,1024]{2,1,0:T(8,128)(2,1)S(1)}, u32[]{:S(2)}, u32[]{:S(2)}) collective-permute-start(bf16[2,8,1024]{2,1,0:T(8,128)(2,1)S(1)} %get-tuple-element.21), channel_id=1, source_target_pairs={{0,32},{1,225},{2,34},{3,227},{4,36},{5,229},{6,38},{7,231},{8,40}... | collective-permute-start | bytes 98312 | tf_op jit(solution)/shard_map/ppermute | solution.py:235
  13.1 4.8 %collective-permute-start.3 = (bf16[2,8,1024]{2,1,0:T(8,128)(2,1)S(1)}, bf16[2,8,1024]{2,1,0:T(8,128)(2,1)S(1)}, u32[]{:S(2)}, u32[]{:S(2)}) collective-permute-start(bf16[2,8,1024]{2,1,0:T(8,128)(2,1)S(1)} %get-tuple-element.22), channel_id=1, source_target_pairs={{0,64},{1,193},{2,66},{3,195},{4,68},{5,197},{6,70},{7,199},{8,72}... | collective-permute-start | bytes 98312 | tf_op jit(solution)/shard_map/ppermute | solution.py:235
  13.2 5.7 %collective-permute-start.4 = (bf16[2,8,1024]{2,1,0:T(8,128)(2,1)S(1)}, bf16[2,8,1024]{2,1,0:T(8,128)(2,1)S(1)}, u32[]{:S(2)}, u32[]{:S(2)}) collective-permute-start(bf16[2,8,1024]{2,1,0:T(8,128)(2,1)S(1)} %get-tuple-element.23), channel_id=1, source_target_pairs={{0,96},{1,161},{2,98},{3,163},{4,100},{5,165},{6,102},{7,167},{8,1... | collective-permute-start | bytes 98312 | tf_op jit(solution)/shard_map/ppermute | solution.py:235
  18.9 6.1 %collective-permute-start.5 = (bf16[8,8,1024]{2,1,0:T(8,128)(2,1)S(1)}, bf16[8,8,1024]{2,1,0:T(8,128)(2,1)S(1)}, u32[]{:S(2)}, u32[]{:S(2)}) collective-permute-start(bf16[8,8,1024]{2,1,0:T(8,128)(2,1)S(1)} %get-tuple-element.26), channel_id=1, source_target_pairs={{0,24},{1,7},{2,26},{3,1},{4,28},{5,3},{6,30},{7,5},{8,0},{9,15},{... | collective-permute-start | bytes 393224 | tf_op jit(solution)/shard_map/ppermute | solution.py:229
  21.7 5.4 %collective-permute-start.6 = (bf16[8,8,1024]{2,1,0:T(8,128)(2,1)S(1)}, bf16[8,8,1024]{2,1,0:T(8,128)(2,1)S(1)}, u32[]{:S(2)}, u32[]{:S(2)}) collective-permute-start(bf16[8,8,1024]{2,1,0:T(8,128)(2,1)S(1)} %get-tuple-element.26), channel_id=1, source_target_pairs={{0,16},{1,5},{2,18},{3,7},{4,20},{5,1},{6,22},{7,3},{8,24},{9,13},... | collective-permute-start | bytes 393224 | tf_op jit(solution)/shard_map/ppermute | solution.py:229
  22.0 6.4 %collective-permute-start.7 = (bf16[8,8,1024]{2,1,0:T(8,128)(2,1)S(1)}, bf16[8,8,1024]{2,1,0:T(8,128)(2,1)S(1)}, u32[]{:S(2)}, u32[]{:S(2)}) collective-permute-start(bf16[8,8,1024]{2,1,0:T(8,128)(2,1)S(1)} %get-tuple-element.26), channel_id=1, source_target_pairs={{0,8},{1,3},{2,10},{3,5},{4,12},{5,7},{6,14},{7,1},{8,16},{9,11},{... | collective-permute-start | bytes 393224 | tf_op jit(solution)/shard_map/ppermute | solution.py:229
  28.4 9.6 %collective-permute-start.11 = (bf16[32,8,1024]{2,1,0:T(8,128)(2,1)S(1)}, bf16[32,8,1024]{2,1,0:T(8,128)(2,1)S(1)}, u32[]{:S(2)}, u32[]{:S(2)}) collective-permute-start(bf16[32,8,1024]{2,1,0:T(8,128)(2,1)S(1)} %constant_dynamic-update-slice_fusion.4.refs_1_), channel_id=1, source_target_pairs={{0,2},{1,9},{2,4},{3,11},{4,6},{5,13},{6,0},{7,15},{8,10},{9,17},{... | collective-permute-start | bytes 1572872 | tf_op jit(solution)/shard_map/ppermute | solution.py:225
  29.7 14.9 %collective-permute-start.10 = (bf16[32,8,1024]{2,1,0:T(8,128)(2,1)S(1)}, bf16[32,8,1024]{2,1,0:T(8,128)(2,1)S(1)}, u32[]{:S(2)}, u32[]{:S(2)}) collective-permute-start(bf16[32,8,1024]{2,1,0:T(8,128)(2,1)S(1)} %constant_dynamic-update-slice_fusion.4.refs_1_), channel_id=1, source_target_pairs={{0,4},{1,17},{2,6},{3,19},{4,0},{5,21},{6,2},{7,23},{8,12},{9,25},... | collective-permute-start | bytes 1572872 | tf_op jit(solution)/shard_map/ppermute | solution.py:225
  32.1 13.1 %collective-permute-start.9 = (bf16[32,8,1024]{2,1,0:T(8,128)(2,1)S(1)}, bf16[32,8,1024]{2,1,0:T(8,128)(2,1)S(1)}, u32[]{:S(2)}, u32[]{:S(2)}) collective-permute-start(bf16[32,8,1024]{2,1,0:T(8,128)(2,1)S(1)} %constant_dynamic-update-slice_fusion.4.refs_1_), channel_id=1, source_target_pairs={{0,6},{1,25},{2,0},{3,27},{4,2},{5,29},{6,4},{7,31},{8,14},{9,1},{... | collective-permute-start | bytes 1572872 | tf_op jit(solution)/shard_map/ppermute | solution.py:225
  33.3 12.0 %collective-permute-start.8 = (bf16[32,8,1024]{2,1,0:T(8,128)(2,1)S(1)}, bf16[32,8,1024]{2,1,0:T(8,128)(2,1)S(1)}, u32[]{:S(2)}, u32[]{:S(2)}) collective-permute-start(bf16[32,8,1024]{2,1,0:T(8,128)(2,1)S(1)} %constant_dynamic-update-slice_fusion.4.refs_1_), channel_id=1, source_target_pairs={{0,1},{1,0},{2,3},{3,2},{4,5},{5,4},{6,7},{7,6},{8,9},{9,8},{10,11... | collective-permute-start | bytes 1572872 | tf_op jit(solution)/shard_map/ppermute | solution.py:225
  38.0 7.3 %collective-permute-start.14 = (bf16[32,8,1024]{2,1,0:T(8,128)(2,1)S(1)}, bf16[32,8,1024]{2,1,0:T(8,128)(2,1)S(1)}, u32[]{:S(2)}, u32[]{:S(2)}) collective-permute-start(bf16[32,8,1024]{2,1,0:T(8,128)(2,1)S(1)} %collective-permute-done.11.refs_5_), channel_id=1, source_target_pairs={{0,1},{1,0},{2,3},{3,2},{4,5},{5,4},{6,7},{7,6},{8,9},{9,8},{10,11... | collective-permute-start | bytes 1572872 | tf_op jit(solution)/shard_map/ppermute | solution.py:225
  44.6 2.2 %collective-permute-start.13 = (bf16[32,8,1024]{2,1,0:T(8,128)(2,1)S(1)}, bf16[32,8,1024]{2,1,0:T(8,128)(2,1)S(1)}, u32[]{:S(2)}, u32[]{:S(2)}) collective-permute-start(bf16[32,8,1024]{2,1,0:T(8,128)(2,1)S(1)} %collective-permute-done.10.refs_4_), channel_id=1, source_target_pairs={{0,1},{1,0},{2,3},{3,2},{4,5},{5,4},{6,7},{7,6},{8,9},{9,8},{10,11... | collective-permute-start | bytes 1572872 | tf_op jit(solution)/shard_map/ppermute | solution.py:225
  45.2 2.3 %collective-permute-start.12 = (bf16[32,8,1024]{2,1,0:T(8,128)(2,1)S(1)}, bf16[32,8,1024]{2,1,0:T(8,128)(2,1)S(1)}, u32[]{:S(2)}, u32[]{:S(2)}) collective-permute-start(bf16[32,8,1024]{2,1,0:T(8,128)(2,1)S(1)} %collective-permute-done.9.refs_3_), channel_id=1, source_target_pairs={{0,1},{1,0},{2,3},{3,2},{4,5},{5,4},{6,7},{7,6},{8,9},{9,8},{10,11... | collective-permute-start | bytes 1572872 | tf_op jit(solution)/shard_map/ppermute | solution.py:225

commit v3 on v2

--- a/solution.py
+++ b/solution.py
@@ -21,6 +21,9 @@
 SEND = 4
 HALF = H_DEV // 2
 WIDE = HALF * DH
+ORDER = (1, 3, 2)
+EARLY = (0, 2, 3)
+LATE = 1
 EPSILON = 1e-06
 AXES = ("head", "rep")
 
@@ -123,44 +126,56 @@
     return messages, rows
 
 
-def absorb_kernel(*refs):
-    far_rows, own_line, other_line = refs[:3]
-    own = refs[3:6]
-    other = refs[6:9]
-    values, scales, rows, placed, scaled, tables, sems, scale_sem, row_sem = refs[9:]
+def place_blocks(rows, pieces, placed):
     at_z = lax.axis_index("head")
     replica = lax.axis_index("rep")
     core = replica & (NC - 1)
     at_x = replica // (NY * NC)
     at_y = (replica // NC) & (NY - 1)
-    fetch = pltpu.make_async_copy(far_rows, rows, row_sem)
+
+    def place(first, carry):
+        for blocks, second, mine in pieces:
+            holder = core if mine else 1 - core
+            x = (at_x + jnp.where(holder == 0, first, second)) & (NX - 1)
+            y = (at_y + jnp.where(holder == 0, second, first)) & (NY - 1)
+            at = x * (NY * NC) + y * NC
+            for step in range(STEPS):
+                z = at_z - jnp.where(holder == 0, z_shift(0, step), z_shift(1, step))
+                for i in range(NC):
+                    row = pl.multiple_of(rows[z & (NZ - 1), at + (holder ^ i)], 8)
+                    index = first * (STEPS * NC) + step * NC + i
+                    block = blocks[index].astype(jnp.float32)
+                    for h in range(H_DEV):
+                        placed[h, pl.ds(row, 8), :] = block[:, h * DH : (h + 1) * DH]
+        return carry
+
+    lax.fori_loop(0, NX, place, 0)
+
+
+def fetch_rows(far_rows, rows, sem):
+    fetch = pltpu.make_async_copy(far_rows, rows, sem)
     fetch.start()
     fetch.wait()
-    for arrays, holder in (((own_line, *own), core), ((other_line, *other), 1 - core)):
-        planes = []
-        for step in range(STEPS):
-            ahead = step if step else NZ // 2
-            planes.append((at_z + jnp.where(holder == 0, NZ - step, ahead)) & (NZ - 1))
-        for second in range(NX):
-
-            def body(first, carry, second=second, planes=planes):
-                x = (at_x + jnp.where(holder == 0, first, second)) & (NX - 1)
-                y = (at_y + jnp.where(holder == 0, second, first)) & (NY - 1)
-                at = x * (NY * NC) + y * NC
-                for step in range(STEPS):
-                    for i in range(NC):
-                        row = pl.multiple_of(rows[planes[step], at + (holder ^ i)], 8)
-                        index = first * (STEPS * NC) + step * NC + i
-                        block = arrays[second][index].astype(jnp.float32)
-                        for h in range(H_DEV):
-                            placed[h, pl.ds(row, 8), :] = block[:, h * DH : (h + 1) * DH]
-                return carry
-
-            lax.fori_loop(0, NX, body, 0)
+
+
+def place_kernel(far_rows, *refs):
+    own, other, (placed, rows, row_sem) = refs[:4], refs[4:-3], refs[-3:]
+    fetch_rows(far_rows, rows, row_sem)
+    pieces = [(blocks, second, True) for second, blocks in zip((0, *ORDER), own, strict=True)]
+    pieces += [(blocks, second, False) for second, blocks in zip(EARLY, other, strict=True)]
+    place_blocks(rows, pieces, placed)
+
+
+def absorb_kernel(far_rows, late, early, values, scales, placed, rows, scaled, tables, *sems):
+    value_sems, scale_sem, row_sem = sems
+    fetch_rows(far_rows, rows, row_sem)
+    place_blocks(rows, [(late, LATE, False)], placed)
 
     def writes(h, k):
         at = pl.ds(k * SEND * QB, SEND * QB)
-        return pltpu.make_async_copy(scaled.at[h, at], values.at[h, at], sems.at[h, k])
+        return pltpu.make_async_copy(
+            scaled.at[h, at], values.at[h, at], value_sems.at[h, k]
+        )
 
     row_at = lax.broadcasted_iota(jnp.int32, (K_BLOCKS, 128), 0)
     col_at = lax.broadcasted_iota(jnp.int32, (K_BLOCKS, 128), 1)
@@ -192,33 +207,45 @@
     finish.wait()
 
 
-def absorb(rows, own_line, other_line, own, other):
+def absorb(rows, own, other):
     vector = pl.BlockSpec(memory_space=pltpu.VMEM)
     anywhere = pl.BlockSpec(memory_space=pl.ANY)
-    return pl.pallas_call(
+    placed = jax.ShapeDtypeStruct((H_DEV, LAT, DH), jnp.float32)
+    fetched = [pltpu.SMEM(rows.shape, rows.dtype)]
+    early = pl.pallas_call(
+        place_kernel,
+        out_shape=placed,
+        in_specs=[vector] * (1 + NX + len(EARLY)),
+        out_specs=vector,
+        scratch_shapes=[*fetched, pltpu.SemaphoreType.DMA],
+        compiler_params=pltpu.CompilerParams(vmem_limit_bytes=4 * 2**20),
+    )(rows, *own.values(), *[other[k] for k in EARLY])
+    values, scales, _ = pl.pallas_call(
         absorb_kernel,
         out_shape=(
             jax.ShapeDtypeStruct((H_DEV, QR, KR), jnp.bfloat16),
             jax.ShapeDtypeStruct((H_DEV, K_BLOCKS, Q_BLOCKS), jnp.bfloat16),
+            placed,
         ),
-        in_specs=[vector] * (3 + len(own) + len(other)),
-        out_specs=(anywhere, anywhere),
+        in_specs=[vector] * 3,
+        out_specs=(anywhere, anywhere, vector),
         scratch_shapes=[
-            pltpu.SMEM(rows.shape, rows.dtype),
-            pltpu.VMEM((H_DEV, LAT, DH), jnp.float32),
+            *fetched,
             pltpu.VMEM((H_DEV, QR, KR), jnp.bfloat16),
             pltpu.VMEM((H_DEV, K_BLOCKS, Q_BLOCKS), jnp.bfloat16),
             pltpu.SemaphoreType.DMA((H_DEV, Q_BLOCKS // SEND)),
             pltpu.SemaphoreType.DMA,
             pltpu.SemaphoreType.DMA,
         ],
-        compiler_params=pltpu.CompilerParams(vmem_limit_bytes=32 * 2**20),
+        input_output_aliases={2: 2},
+        compiler_params=pltpu.CompilerParams(vmem_limit_bytes=20 * 2**20),
         cost_estimate=pl.CostEstimate(
             flops=2 * H_DEV * QR * KR * DH,
             bytes_accessed=H_DEV * QR * KR * 2,
             transcendentals=0,
         ),
-    )(rows, own_line, other_line, *own, *other)
+    )(rows, other[LATE], early)
+    return values, scales
 
 
 def move(block, target):
@@ -235,10 +262,9 @@
         [lax.ppermute(m, AXES, along_z(s)) for s, m in enumerate(messages)]
     )
     line = jnp.concatenate(gather_phase(arrived, first_axis))
-    own = [move(line, second_axis(k)) for k in (1, 2, 3)]
-    other = [move(piece, other_core()) for piece in own]
-    other_line = move(line, other_core())
-    values, scales = absorb(rows, line, other_line, own, other)
+    own = {0: line} | {k: move(line, second_axis(k)) for k in ORDER}
+    other = {k: move(piece, other_core()) for k, piece in own.items()}
+    values, scales = absorb(rows, own, other)
     return values, scales.transpose(0, 2, 1)
 
 

time: 55.4 us -> 54.5 us (0.984)
  waiting for transfers between devices: 19.3 us -> 16.8 us
  starting transfers between devices: 25.4 us -> 26.3 us
  Pallas kernels: 7.6 us -> 8.2 us
    ppermute x8, waiting for transfers between devices: 12.7 us -> 10.2 us  [move(): return lax.ppermute(block, AXES, target)]
    pallas_call x0 -> x1, Pallas kernels: none -> 1.42 us  [absorb(): pl.pallas_call(place_kernel, out_shape=placed, in_specs=[vector] * (1 + N...]
    ppermute x8, starting transfers between devices: 9.76 us -> 10.6 us  [move(): return lax.ppermute(block, AXES, target)]
    pallas_call x1, Pallas kernels: 7.36 us -> 6.54 us  [absorb(): pl.pallas_call(absorb_kernel, out_shape=(jax.ShapeDtypeStruct((H_DEV, QR,...]
  transfers between devices with their start and end apart: 15 -> 15, of which waited for: 8 -> 7; matrix products, arithmetic and copies ran while one was open for 0% -> 0% of each run, Pallas kernels for 0% -> 3%
where the time goes in v3:
time: 54.5 us; the launch traced here: 54 us
  starting transfers between devices  26.3 us (48%)
  waiting for transfers between devices  16.8 us (31%)
  Pallas kernels  8.2 us (15%)
  local copies, waits for them, and re-layouts  1.8 us (3%)
  between operations  0.91 us (2%)
    ppermute x4, starting transfers between devices, on_device(): lax.ppermute(m, AXES, along_z(s))  11.9 us
    ppermute x8, starting transfers between devices, move(): return lax.ppermute(block, AXES, target)  10.6 us
    ppermute x8, waiting for transfers between devices, move(): return lax.ppermute(block, AXES, target)  10.2 us
    pallas_call x1, Pallas kernels, absorb(): pl.pallas_call(absorb_kernel, out_shape=(jax.ShapeDtypeStruct((H_DEV, QR,...  6.54 us
    ppermute x3, waiting for transfers between devices, gather_phase(): return [block] + [lax.ppermute(block, AXES, target(k)) for k in (1, 2, 3)]  5.66 us
    ppermute x3, starting transfers between devices, gather_phase(): return [block] + [lax.ppermute(block, AXES, target(k)) for k in (1, 2, 3)]  3.77 us
    unnamed x9, local copies, waits for them, and re-layouts  1.78 us
    pallas_call x1, Pallas kernels, absorb(): pl.pallas_call(place_kernel, out_shape=placed, in_specs=[vector] * (1 + N...  1.42 us
  transfers between devices with their start and end apart: 15, of which 7 were waited for; matrix products, arithmetic and copies ran while one was open for 0% of the time, Pallas kernels for 3%

profile of v3, /device:TPU:1, one launch (start us, length us, event | category | flops | bytes accessed | tf_op | source)
XLA Modules:
  0.0 54.0 jit_solution(642821078161731317)
XLA Ops:
  0.6 3.3 %collective-permute-start = (bf16[8,8,1024]{2,1,0:T(8,128)(2,1)}, bf16[8,8,1024]{2,1,0:T(8,128)(2,1)S(1)}, u32[]{:S(2)}, u32[]{:S(2)}) collective-permute-start(bf16[8,8,1024]{2,1,0:T(8,128)(2,1)} %bitcast.3), channel_id=1, source_target_pairs={{0,1},{1,0},{2,3},{3,2},{4,5},{5,4},{6,7},{7,6},{8,9},{9,8},{10,11... | collective-permute-start | bytes 393224 | tf_op jit(solution)/shard_map/ppermute | solution.py:252
  4.0 0.9 %copy-done = bf16[1,1,8,8,1024]{4,3,2,1,0:T(8,128)(2,1)S(1)} copy-done((bf16[1,1,8,8,1024]{4,3,2,1,0:T(8,128)(2,1)S(1)}, bf16[1,1,8,8,1024]{4,3,2,1,0:T(8,128)(2,1)}, u32[]{:S(2)}) %copy-start) | copy-done | bytes 131096
  4.9 0.8 %copy-done.1 = s32[8,32,8,2]{1,3,2,0:T(2,128)S(1)} copy-done((s32[8,32,8,2]{1,3,2,0:T(2,128)S(1)}, s32[8,32,8,2]{1,3,2,0:T(2,128)}, u32[]{:S(2)}) %copy-start.1) | copy-done | bytes 16408
  6.0 7.1 %collective-permute-start.1 = (bf16[2,8,1024]{2,1,0:T(8,128)(2,1)S(1)}, bf16[2,8,1024]{2,1,0:T(8,128)(2,1)S(1)}, u32[]{:S(2)}, u32[]{:S(2)}) collective-permute-start(bf16[2,8,1024]{2,1,0:T(8,128)(2,1)S(1)} %get-tuple-element.20), channel_id=1, source_target_pairs={{0,0},{1,129},{2,2},{3,131},{4,4},{5,133},{6,6},{7,135},{8,8},{9,1... | collective-permute-start | bytes 98312 | tf_op jit(solution)/shard_map/ppermute | solution.py:262
  13.2 4.7 %collective-permute-start.4 = (bf16[2,8,1024]{2,1,0:T(8,128)(2,1)S(1)}, bf16[2,8,1024]{2,1,0:T(8,128)(2,1)S(1)}, u32[]{:S(2)}, u32[]{:S(2)}) collective-permute-start(bf16[2,8,1024]{2,1,0:T(8,128)(2,1)S(1)} %get-tuple-element.23), channel_id=1, source_target_pairs={{0,96},{1,161},{2,98},{3,163},{4,100},{5,165},{6,102},{7,167},{8,1... | collective-permute-start | bytes 98312 | tf_op jit(solution)/shard_map/ppermute | solution.py:262
  18.0 1.0 %collective-permute-done.4 = bf16[2,8,1024]{2,1,0:T(8,128)(2,1)S(1)} collective-permute-done((bf16[2,8,1024]{2,1,0:T(8,128)(2,1)S(1)}, bf16[2,8,1024]{2,1,0:T(8,128)(2,1)S(1)}, u32[]{:S(2)}, u32[]{:S(2)}) %collective-permute-start.4) | collective-permute-done | bytes 32800 | tf_op jit(solution)/shard_map/ppermute | solution.py:262
  18.9 2.7 %collective-permute-start.5 = (bf16[8,8,1024]{2,1,0:T(8,128)(2,1)S(1)}, bf16[8,8,1024]{2,1,0:T(8,128)(2,1)S(1)}, u32[]{:S(2)}, u32[]{:S(2)}) collective-permute-start(bf16[8,8,1024]{2,1,0:T(8,128)(2,1)S(1)} %get-tuple-element.26), channel_id=1, source_target_pairs={{0,24},{1,7},{2,26},{3,1},{4,28},{5,3},{6,30},{7,5},{8,0},{9,15},{... | collective-permute-start | bytes 393224 | tf_op jit(solution)/shard_map/ppermute | solution.py:256
  21.7 0.3 collective-permute-start.6
  22.0 0.7 %collective-permute-start.7 = (bf16[8,8,1024]{2,1,0:T(8,128)(2,1)S(1)}, bf16[8,8,1024]{2,1,0:T(8,128)(2,1)S(1)}, u32[]{:S(2)}, u32[]{:S(2)}) collective-permute-start(bf16[8,8,1024]{2,1,0:T(8,128)(2,1)S(1)} %get-tuple-element.26), channel_id=1, source_target_pairs={{0,8},{1,3},{2,10},{3,5},{4,12},{5,7},{6,14},{7,1},{8,16},{9,11},{... | collective-permute-start | bytes 393224 | tf_op jit(solution)/shard_map/ppermute | solution.py:256
  22.7 2.3 %collective-permute-done.5 = bf16[8,8,1024]{2,1,0:T(8,128)(2,1)S(1)} collective-permute-done((bf16[8,8,1024]{2,1,0:T(8,128)(2,1)S(1)}, bf16[8,8,1024]{2,1,0:T(8,128)(2,1)S(1)}, u32[]{:S(2)}, u32[]{:S(2)}) %collective-permute-start.5) | collective-permute-done | bytes 131104 | tf_op jit(solution)/shard_map/ppermute | solution.py:256
  25.0 2.1 %collective-permute-done.6 = bf16[8,8,1024]{2,1,0:T(8,128)(2,1)S(1)} collective-permute-done((bf16[8,8,1024]{2,1,0:T(8,128)(2,1)S(1)}, bf16[8,8,1024]{2,1,0:T(8,128)(2,1)S(1)}, u32[]{:S(2)}, u32[]{:S(2)}) %collective-permute-start.6) | collective-permute-done | bytes 131104 | tf_op jit(solution)/shard_map/ppermute | solution.py:256
  27.1 1.3 %collective-permute-done.7 = bf16[8,8,1024]{2,1,0:T(8,128)(2,1)S(1)} collective-permute-done((bf16[8,8,1024]{2,1,0:T(8,128)(2,1)S(1)}, bf16[8,8,1024]{2,1,0:T(8,128)(2,1)S(1)}, u32[]{:S(2)}, u32[]{:S(2)}) %collective-permute-start.7) | collective-permute-done | bytes 131104 | tf_op jit(solution)/shard_map/ppermute | solution.py:256
  28.4 2.8 %collective-permute-start.11 = (bf16[32,8,1024]{2,1,0:T(8,128)(2,1)S(1)}, bf16[32,8,1024]{2,1,0:T(8,128)(2,1)S(1)}, u32[]{:S(2)}, u32[]{:S(2)}) collective-permute-start(bf16[32,8,1024]{2,1,0:T(8,128)(2,1)S(1)} %constant_dynamic-update-slice_fusion.4.refs_0_), channel_id=1, source_target_pairs={{0,4},{1,17},{2,6},{3,19},{4,0},{5,21},{6,2},{7,23},{8,12},{9,25},... | collective-permute-start | bytes 1572872 | tf_op jit(solution)/shard_map/ppermute | solution.py:252
  31.2 0.3 collective-permute-start.10
  31.5 2.4 %collective-permute-start.8 = (bf16[32,8,1024]{2,1,0:T(8,128)(2,1)S(1)}, bf16[32,8,1024]{2,1,0:T(8,128)(2,1)S(1)}, u32[]{:S(2)}, u32[]{:S(2)}) collective-permute-start(bf16[32,8,1024]{2,1,0:T(8,128)(2,1)S(1)} %constant_dynamic-update-slice_fusion.4.refs_0_), channel_id=1, source_target_pairs={{0,6},{1,25},{2,0},{3,27},{4,2},{5,29},{6,4},{7,31},{8,14},{9,1},{... | collective-permute-start | bytes 1572872 | tf_op jit(solution)/shard_map/ppermute | solution.py:252
  33.9 0.5 collective-permute-start.12
  34.4 3.9 %collective-permute-done.11.refs_3_ = bf16[32,8,1024]{2,1,0:T(8,128)(2,1)S(1)} collective-permute-done((bf16[32,8,1024]{2,1,0:T(8,128)(2,1)S(1)}, bf16[32,8,1024]{2,1,0:T(8,128)(2,1)S(1)}, u32[]{:S(2)}, u32[]{:S(2)}) %collective-permute-start.11) | collective-permute-done | bytes 524320 | tf_op jit(solution)/shard_map/ppermute | solution.py:252
  38.3 0.5 collective-permute-start.13
  38.8 5.1 %collective-permute-done.10.refs_2_ = bf16[32,8,1024]{2,1,0:T(8,128)(2,1)S(1)} collective-permute-done((bf16[32,8,1024]{2,1,0:T(8,128)(2,1)S(1)}, bf16[32,8,1024]{2,1,0:T(8,128)(2,1)S(1)}, u32[]{:S(2)}, u32[]{:S(2)}) %collective-permute-start.10) | collective-permute-done | bytes 524320 | tf_op jit(solution)/shard_map/ppermute | solution.py:252
  43.9 0.4 collective-permute-start.14
  44.3 0.4 collective-permute-start.9
  44.7 1.1 %collective-permute-done.14.refs_6_ = bf16[32,8,1024]{2,1,0:T(8,128)(2,1)S(1)} collective-permute-done((bf16[32,8,1024]{2,1,0:T(8,128)(2,1)S(1)}, bf16[32,8,1024]{2,1,0:T(8,128)(2,1)S(1)}, u32[]{:S(2)}, u32[]{:S(2)}) %collective-permute-start.14) | collective-permute-done | bytes 524320 | tf_op jit(solution)/shard_map/ppermute | solution.py:252
  45.8 1.4 %shard_map.43.early = f32[8,2048,128]{2,1,0:T(8,128)S(1)} custom-call(s32[8,32]{1,0:T(8,128)S(1)} %get-tuple-element.14.far_rows, bf16[32,8,1024]{2,1,0:T(8,128)(2,1)S(1)} %constant_dynamic-update-slice_fusion.4.refs_0_, bf16[32,8,1024]{2,1,0:T(8,128)(2,1)S(1)} %collective-permute-done.8.refs_1_, bf16[32,8,1024]{2,1,0:T(8,128)(2,1)S(1)} %collective-permute-done.10.refs_2_, ...), custom_call_target="tpu_custom_call" | custom-call | tf_op jit(solution)/shard_map/pallas_call | solution.py:215
  47.3 6.5 %shard_map.44 = (bf16[8,1536,512]{2,1,0:T(8,128)(2,1)}, bf16[8,4,12]{2,1,0:T(4,128)(2,1)}, f32[8,2048,128]{2,1,0:T(8,128)S(1)}) custom-call(s32[8,32]{1,0:T(8,128)S(1)} %get-tuple-element.14.far_rows, bf16[32,8,1024]{2,1,0:T(8,128)(2,1)S(1)} %collective-permute-done.9.late, f32[8,2048,128]{2,1,0:T(8,128)S(1)} %shard_map.43.early), custom_call_target="tpu_custom_call", output_to_operand_aliasing={{2}: (2, {})} | custom-call | flops 1610612736 | bytes 12582912 | tf_op jit(solution)/shard_map/pallas_call | solution.py:223
  (21 shorter events, 0.5 us)
Async XLA Ops:
  0.6 5.2 %collective-permute-start = (bf16[8,8,1024]{2,1,0:T(8,128)(2,1)}, bf16[8,8,1024]{2,1,0:T(8,128)(2,1)S(1)}, u32[]{:S(2)}, u32[]{:S(2)}) collective-permute-start(bf16[8,8,1024]{2,1,0:T(8,128)(2,1)} %bitcast.3), channel_id=1, source_target_pairs={{0,1},{1,0},{2,3},{3,2},{4,5},{5,4},{6,7},{7,6},{8,9},{9,8},{10,11... | collective-permute-start | bytes 393224 | tf_op jit(solution)/shard_map/ppermute | solution.py:252
  4.0 0.9 %copy-start = (bf16[1,1,8,8,1024]{4,3,2,1,0:T(8,128)(2,1)S(1)}, bf16[1,1,8,8,1024]{4,3,2,1,0:T(8,128)(2,1)}, u32[]{:S(2)}) copy-start(bf16[1,1,8,8,1024]{4,3,2,1,0:T(8,128)(2,1)} %param.2) | copy-start | bytes 393220
  4.9 0.8 %copy-start.1 = (s32[8,32,8,2]{1,3,2,0:T(2,128)S(1)}, s32[8,32,8,2]{1,3,2,0:T(2,128)}, u32[]{:S(2)}) copy-start(s32[8,32,8,2]{1,3,2,0:T(2,128)} %param.3) | copy-start | bytes 49156
  6.0 11.9 %collective-permute-start.1 = (bf16[2,8,1024]{2,1,0:T(8,128)(2,1)S(1)}, bf16[2,8,1024]{2,1,0:T(8,128)(2,1)S(1)}, u32[]{:S(2)}, u32[]{:S(2)}) collective-permute-start(bf16[2,8,1024]{2,1,0:T(8,128)(2,1)S(1)} %get-tuple-element.20), channel_id=1, source_target_pairs={{0,0},{1,129},{2,2},{3,131},{4,4},{5,133},{6,6},{7,135},{8,8},{9,1... | collective-permute-start | bytes 98312 | tf_op jit(solution)/shard_map/ppermute | solution.py:262
  13.0 4.9 %collective-permute-start.2 = (bf16[2,8,1024]{2,1,0:T(8,128)(2,1)S(1)}, bf16[2,8,1024]{2,1,0:T(8,128)(2,1)S(1)}, u32[]{:S(2)}, u32[]{:S(2)}) collective-permute-start(bf16[2,8,1024]{2,1,0:T(8,128)(2,1)S(1)} %get-tuple-element.21), channel_id=1, source_target_pairs={{0,32},{1,225},{2,34},{3,227},{4,36},{5,229},{6,38},{7,231},{8,40}... | collective-permute-start | bytes 98312 | tf_op jit(solution)/shard_map/ppermute | solution.py:262
  13.1 4.8 %collective-permute-start.3 = (bf16[2,8,1024]{2,1,0:T(8,128)(2,1)S(1)}, bf16[2,8,1024]{2,1,0:T(8,128)(2,1)S(1)}, u32[]{:S(2)}, u32[]{:S(2)}) collective-permute-start(bf16[2,8,1024]{2,1,0:T(8,128)(2,1)S(1)} %get-tuple-element.22), channel_id=1, source_target_pairs={{0,64},{1,193},{2,66},{3,195},{4,68},{5,197},{6,70},{7,199},{8,72}... | collective-permute-start | bytes 98312 | tf_op jit(solution)/shard_map/ppermute | solution.py:262
  13.2 5.7 %collective-permute-start.4 = (bf16[2,8,1024]{2,1,0:T(8,128)(2,1)S(1)}, bf16[2,8,1024]{2,1,0:T(8,128)(2,1)S(1)}, u32[]{:S(2)}, u32[]{:S(2)}) collective-permute-start(bf16[2,8,1024]{2,1,0:T(8,128)(2,1)S(1)} %get-tuple-element.23), channel_id=1, source_target_pairs={{0,96},{1,161},{2,98},{3,163},{4,100},{5,165},{6,102},{7,167},{8,1... | collective-permute-start | bytes 98312 | tf_op jit(solution)/shard_map/ppermute | solution.py:262
  18.9 6.1 %collective-permute-start.5 = (bf16[8,8,1024]{2,1,0:T(8,128)(2,1)S(1)}, bf16[8,8,1024]{2,1,0:T(8,128)(2,1)S(1)}, u32[]{:S(2)}, u32[]{:S(2)}) collective-permute-start(bf16[8,8,1024]{2,1,0:T(8,128)(2,1)S(1)} %get-tuple-element.26), channel_id=1, source_target_pairs={{0,24},{1,7},{2,26},{3,1},{4,28},{5,3},{6,30},{7,5},{8,0},{9,15},{... | collective-permute-start | bytes 393224 | tf_op jit(solution)/shard_map/ppermute | solution.py:256
  21.7 5.4 %collective-permute-start.6 = (bf16[8,8,1024]{2,1,0:T(8,128)(2,1)S(1)}, bf16[8,8,1024]{2,1,0:T(8,128)(2,1)S(1)}, u32[]{:S(2)}, u32[]{:S(2)}) collective-permute-start(bf16[8,8,1024]{2,1,0:T(8,128)(2,1)S(1)} %get-tuple-element.26), channel_id=1, source_target_pairs={{0,16},{1,5},{2,18},{3,7},{4,20},{5,1},{6,22},{7,3},{8,24},{9,13},... | collective-permute-start | bytes 393224 | tf_op jit(solution)/shard_map/ppermute | solution.py:256
  22.0 6.4 %collective-permute-start.7 = (bf16[8,8,1024]{2,1,0:T(8,128)(2,1)S(1)}, bf16[8,8,1024]{2,1,0:T(8,128)(2,1)S(1)}, u32[]{:S(2)}, u32[]{:S(2)}) collective-permute-start(bf16[8,8,1024]{2,1,0:T(8,128)(2,1)S(1)} %get-tuple-element.26), channel_id=1, source_target_pairs={{0,8},{1,3},{2,10},{3,5},{4,12},{5,7},{6,14},{7,1},{8,16},{9,11},{... | collective-permute-start | bytes 393224 | tf_op jit(solution)/shard_map/ppermute | solution.py:256
  28.4 9.9 %collective-permute-start.11 = (bf16[32,8,1024]{2,1,0:T(8,128)(2,1)S(1)}, bf16[32,8,1024]{2,1,0:T(8,128)(2,1)S(1)}, u32[]{:S(2)}, u32[]{:S(2)}) collective-permute-start(bf16[32,8,1024]{2,1,0:T(8,128)(2,1)S(1)} %constant_dynamic-update-slice_fusion.4.refs_0_), channel_id=1, source_target_pairs={{0,4},{1,17},{2,6},{3,19},{4,0},{5,21},{6,2},{7,23},{8,12},{9,25},... | collective-permute-start | bytes 1572872 | tf_op jit(solution)/shard_map/ppermute | solution.py:252
  31.2 12.7 %collective-permute-start.10 = (bf16[32,8,1024]{2,1,0:T(8,128)(2,1)S(1)}, bf16[32,8,1024]{2,1,0:T(8,128)(2,1)S(1)}, u32[]{:S(2)}, u32[]{:S(2)}) collective-permute-start(bf16[32,8,1024]{2,1,0:T(8,128)(2,1)S(1)} %constant_dynamic-update-slice_fusion.4.refs_0_), channel_id=1, source_target_pairs={{0,2},{1,9},{2,4},{3,11},{4,6},{5,13},{6,0},{7,15},{8,10},{9,17},{... | collective-permute-start | bytes 1572872 | tf_op jit(solution)/shard_map/ppermute | solution.py:252
  31.5 12.8 %collective-permute-start.8 = (bf16[32,8,1024]{2,1,0:T(8,128)(2,1)S(1)}, bf16[32,8,1024]{2,1,0:T(8,128)(2,1)S(1)}, u32[]{:S(2)}, u32[]{:S(2)}) collective-permute-start(bf16[32,8,1024]{2,1,0:T(8,128)(2,1)S(1)} %constant_dynamic-update-slice_fusion.4.refs_0_), channel_id=1, source_target_pairs={{0,6},{1,25},{2,0},{3,27},{4,2},{5,29},{6,4},{7,31},{8,14},{9,1},{... | collective-permute-start | bytes 1572872 | tf_op jit(solution)/shard_map/ppermute | solution.py:252
  33.9 10.8 %collective-permute-start.12 = (bf16[32,8,1024]{2,1,0:T(8,128)(2,1)S(1)}, bf16[32,8,1024]{2,1,0:T(8,128)(2,1)S(1)}, u32[]{:S(2)}, u32[]{:S(2)}) collective-permute-start(bf16[32,8,1024]{2,1,0:T(8,128)(2,1)S(1)} %constant_dynamic-update-slice_fusion.4.refs_0_), channel_id=1, source_target_pairs={{0,1},{1,0},{2,3},{3,2},{4,5},{5,4},{6,7},{7,6},{8,9},{9,8},{10,11... | collective-permute-start | bytes 1572872 | tf_op jit(solution)/shard_map/ppermute | solution.py:252
  38.3 6.4 %collective-permute-start.13 = (bf16[32,8,1024]{2,1,0:T(8,128)(2,1)S(1)}, bf16[32,8,1024]{2,1,0:T(8,128)(2,1)S(1)}, u32[]{:S(2)}, u32[]{:S(2)}) collective-permute-start(bf16[32,8,1024]{2,1,0:T(8,128)(2,1)S(1)} %collective-permute-done.11.refs_3_), channel_id=1, source_target_pairs={{0,1},{1,0},{2,3},{3,2},{4,5},{5,4},{6,7},{7,6},{8,9},{9,8},{10,11... | collective-permute-start | bytes 1572872 | tf_op jit(solution)/shard_map/ppermute | solution.py:252
  43.9 1.9 %collective-permute-start.14 = (bf16[32,8,1024]{2,1,0:T(8,128)(2,1)S(1)}, bf16[32,8,1024]{2,1,0:T(8,128)(2,1)S(1)}, u32[]{:S(2)}, u32[]{:S(2)}) collective-permute-start(bf16[32,8,1024]{2,1,0:T(8,128)(2,1)S(1)} %collective-permute-done.10.refs_2_), channel_id=1, source_target_pairs={{0,1},{1,0},{2,3},{3,2},{4,5},{5,4},{6,7},{7,6},{8,9},{9,8},{10,11... | collective-permute-start | bytes 1572872 | tf_op jit(solution)/shard_map/ppermute | solution.py:252
  44.3 3.0 %collective-permute-start.9 = (bf16[32,8,1024]{2,1,0:T(8,128)(2,1)S(1)}, bf16[32,8,1024]{2,1,0:T(8,128)(2,1)S(1)}, u32[]{:S(2)}, u32[]{:S(2)}) collective-permute-start(bf16[32,8,1024]{2,1,0:T(8,128)(2,1)S(1)} %collective-permute-done.8.refs_1_), channel_id=1, source_target_pairs={{0,1},{1,0},{2,3},{3,2},{4,5},{5,4},{6,7},{7,6},{8,9},{9,8},{10,11... | collective-permute-start | bytes 1572872 | tf_op jit(solution)/shard_map/ppermute | solution.py:252

commit v4 on v3

--- a/solution.py
+++ b/solution.py
@@ -134,10 +134,11 @@
     at_y = (replica // NC) & (NY - 1)
 
     def place(first, carry):
+        offset = (NX - first) & (NX - 1)
         for blocks, second, mine in pieces:
             holder = core if mine else 1 - core
-            x = (at_x + jnp.where(holder == 0, first, second)) & (NX - 1)
-            y = (at_y + jnp.where(holder == 0, second, first)) & (NY - 1)
+            x = (at_x + jnp.where(holder == 0, offset, second)) & (NX - 1)
+            y = (at_y + jnp.where(holder == 0, second, offset)) & (NY - 1)
             at = x * (NY * NC) + y * NC
             for step in range(STEPS):
                 z = at_z - jnp.where(holder == 0, z_shift(0, step), z_shift(1, step))
@@ -252,16 +253,12 @@
     return lax.ppermute(block, AXES, target)
 
 
-def gather_phase(block, target):
-    return [block] + [lax.ppermute(block, AXES, target(k)) for k in (1, 2, 3)]
-
-
 def on_device(trainer_rows, route):
     messages, rows = prepare(trainer_rows[0, 0], route)
     arrived = jnp.concatenate(
         [lax.ppermute(m, AXES, along_z(s)) for s, m in enumerate(messages)]
     )
-    line = jnp.concatenate(gather_phase(arrived, first_axis))
+    line = jnp.concatenate([arrived] + [move(arrived, first_axis(k)) for k in (3, 2, 1)])
     own = {0: line} | {k: move(line, second_axis(k)) for k in ORDER}
     other = {k: move(piece, other_core()) for k, piece in own.items()}
     values, scales = absorb(rows, own, other)

time: 54.5 us -> 53.1 us (0.974)
  waiting for transfers between devices: 16.8 us -> 13.4 us
  starting transfers between devices: 26.3 us -> 28.3 us
    ppermute x8 -> x11, starting transfers between devices: 10.6 us -> 16.4 us  [move(): return lax.ppermute(block, AXES, target)]
    ppermute x3 -> x0, waiting for transfers between devices: 5.66 us -> none  [gather_phase(): return [block] + [lax.ppermute(block, AXES, target(k)) for k in (1, 2, 3)]]
    ppermute x3 -> x0, starting transfers between devices: 3.77 us -> none  [gather_phase(): return [block] + [lax.ppermute(block, AXES, target(k)) for k in (1, 2, 3)]]
    ppermute x8 -> x11, waiting for transfers between devices: 10.2 us -> 12.4 us  [move(): return lax.ppermute(block, AXES, target)]
  transfers between devices with their start and end apart: 15 -> 15, of which waited for: 7 -> 6; matrix products, arithmetic and copies ran while one was open for 0% -> 0% of each run, Pallas kernels for 3% -> 3%
where the time goes in v4:
time: 53.1 us; the launch traced here: 52.5 us
  starting transfers between devices  28.3 us (53%)
  waiting for transfers between devices  13.4 us (25%)
  Pallas kernels  8.21 us (15%)
  local copies, waits for them, and re-layouts  1.8 us (3%)
  between operations  0.91 us (2%)
    ppermute x11, starting transfers between devices, move(): return lax.ppermute(block, AXES, target)  16.4 us
    ppermute x11, waiting for transfers between devices, move(): return lax.ppermute(block, AXES, target)  12.4 us
    ppermute x4, starting transfers between devices, on_device(): lax.ppermute(m, AXES, along_z(s))  11.9 us
    pallas_call x1, Pallas kernels, absorb(): pl.pallas_call(absorb_kernel, out_shape=(jax.ShapeDtypeStruct((H_DEV, QR,...  6.54 us
    unnamed x9, local copies, waits for them, and re-layouts  1.78 us
    pallas_call x1, Pallas kernels, absorb(): pl.pallas_call(place_kernel, out_shape=placed, in_specs=[vector] * (1 + N...  1.44 us
  transfers between devices with their start and end apart: 15, of which 6 were waited for; matrix products, arithmetic and copies ran while one was open for 0% of the time, Pallas kernels for 3%

profile of v4, /device:TPU:1, one launch (start us, length us, event | category | flops | bytes accessed | tf_op | source)
XLA Modules:
  0.0 52.5 jit_solution(9572490527657716868)
XLA Ops:
  0.6 3.3 %collective-permute-start = (bf16[8,8,1024]{2,1,0:T(8,128)(2,1)}, bf16[8,8,1024]{2,1,0:T(8,128)(2,1)S(1)}, u32[]{:S(2)}, u32[]{:S(2)}) collective-permute-start(bf16[8,8,1024]{2,1,0:T(8,128)(2,1)} %bitcast.3), channel_id=1, source_target_pairs={{0,1},{1,0},{2,3},{3,2},{4,5},{5,4},{6,7},{7,6},{8,9},{9,8},{10,11... | collective-permute-start | bytes 393224 | tf_op jit(solution)/shard_map/ppermute | solution.py:253
  4.0 0.9 %copy-done = bf16[1,1,8,8,1024]{4,3,2,1,0:T(8,128)(2,1)S(1)} copy-done((bf16[1,1,8,8,1024]{4,3,2,1,0:T(8,128)(2,1)S(1)}, bf16[1,1,8,8,1024]{4,3,2,1,0:T(8,128)(2,1)}, u32[]{:S(2)}) %copy-start) | copy-done | bytes 131096
  4.9 0.8 %copy-done.1 = s32[8,32,8,2]{1,3,2,0:T(2,128)S(1)} copy-done((s32[8,32,8,2]{1,3,2,0:T(2,128)S(1)}, s32[8,32,8,2]{1,3,2,0:T(2,128)}, u32[]{:S(2)}) %copy-start.1) | copy-done | bytes 16408
  5.7 0.1 shard_map.41
  6.0 7.1 %collective-permute-start.1 = (bf16[2,8,1024]{2,1,0:T(8,128)(2,1)S(1)}, bf16[2,8,1024]{2,1,0:T(8,128)(2,1)S(1)}, u32[]{:S(2)}, u32[]{:S(2)}) collective-permute-start(bf16[2,8,1024]{2,1,0:T(8,128)(2,1)S(1)} %get-tuple-element.20), channel_id=1, source_target_pairs={{0,0},{1,129},{2,2},{3,131},{4,4},{5,133},{6,6},{7,135},{8,8},{9,1... | collective-permute-start | bytes 98312 | tf_op jit(solution)/shard_map/ppermute | solution.py:259
  13.2 4.7 %collective-permute-start.4 = (bf16[2,8,1024]{2,1,0:T(8,128)(2,1)S(1)}, bf16[2,8,1024]{2,1,0:T(8,128)(2,1)S(1)}, u32[]{:S(2)}, u32[]{:S(2)}) collective-permute-start(bf16[2,8,1024]{2,1,0:T(8,128)(2,1)S(1)} %get-tuple-element.23), channel_id=1, source_target_pairs={{0,96},{1,161},{2,98},{3,163},{4,100},{5,165},{6,102},{7,167},{8,1... | collective-permute-start | bytes 98312 | tf_op jit(solution)/shard_map/ppermute | solution.py:259
  18.0 1.0 %collective-permute-done.4 = bf16[2,8,1024]{2,1,0:T(8,128)(2,1)S(1)} collective-permute-done((bf16[2,8,1024]{2,1,0:T(8,128)(2,1)S(1)}, bf16[2,8,1024]{2,1,0:T(8,128)(2,1)S(1)}, u32[]{:S(2)}, u32[]{:S(2)}) %collective-permute-start.4) | collective-permute-done | bytes 32800 | tf_op jit(solution)/shard_map/ppermute | solution.py:259
  18.9 1.3 %collective-permute-start.5 = (bf16[8,8,1024]{2,1,0:T(8,128)(2,1)S(1)}, bf16[8,8,1024]{2,1,0:T(8,128)(2,1)S(1)}, u32[]{:S(2)}, u32[]{:S(2)}) collective-permute-start(bf16[8,8,1024]{2,1,0:T(8,128)(2,1)S(1)} %get-tuple-element.26), channel_id=1, source_target_pairs={{0,8},{1,3},{2,10},{3,5},{4,12},{5,7},{6,14},{7,1},{8,16},{9,11},{... | collective-permute-start | bytes 393224 | tf_op jit(solution)/shard_map/ppermute | solution.py:253
  20.2 2.6 %collective-permute-start.6 = (bf16[8,8,1024]{2,1,0:T(8,128)(2,1)S(1)}, bf16[8,8,1024]{2,1,0:T(8,128)(2,1)S(1)}, u32[]{:S(2)}, u32[]{:S(2)}) collective-permute-start(bf16[8,8,1024]{2,1,0:T(8,128)(2,1)S(1)} %get-tuple-element.26), channel_id=1, source_target_pairs={{0,16},{1,5},{2,18},{3,7},{4,20},{5,1},{6,22},{7,3},{8,24},{9,13},... | collective-permute-start | bytes 393224 | tf_op jit(solution)/shard_map/ppermute | solution.py:253
  22.8 1.1 %collective-permute-start.7 = (bf16[8,8,1024]{2,1,0:T(8,128)(2,1)S(1)}, bf16[8,8,1024]{2,1,0:T(8,128)(2,1)S(1)}, u32[]{:S(2)}, u32[]{:S(2)}) collective-permute-start(bf16[8,8,1024]{2,1,0:T(8,128)(2,1)S(1)} %get-tuple-element.26), channel_id=1, source_target_pairs={{0,24},{1,7},{2,26},{3,1},{4,28},{5,3},{6,30},{7,5},{8,0},{9,15},{... | collective-permute-start | bytes 393224 | tf_op jit(solution)/shard_map/ppermute | solution.py:253
  23.9 0.4 collective-permute-done.5
  24.3 2.3 %collective-permute-done.6 = bf16[8,8,1024]{2,1,0:T(8,128)(2,1)S(1)} collective-permute-done((bf16[8,8,1024]{2,1,0:T(8,128)(2,1)S(1)}, bf16[8,8,1024]{2,1,0:T(8,128)(2,1)S(1)}, u32[]{:S(2)}, u32[]{:S(2)}) %collective-permute-start.6) | collective-permute-done | bytes 131104 | tf_op jit(solution)/shard_map/ppermute | solution.py:253
  26.7 2.8 %collective-permute-start.11 = (bf16[32,8,1024]{2,1,0:T(8,128)(2,1)S(1)}, bf16[32,8,1024]{2,1,0:T(8,128)(2,1)S(1)}, u32[]{:S(2)}, u32[]{:S(2)}) collective-permute-start(bf16[32,8,1024]{2,1,0:T(8,128)(2,1)S(1)} %constant_dynamic-update-slice_fusion.4.refs_0_), channel_id=1, source_target_pairs={{0,4},{1,17},{2,6},{3,19},{4,0},{5,21},{6,2},{7,23},{8,12},{9,25},... | collective-permute-start | bytes 1572872 | tf_op jit(solution)/shard_map/ppermute | solution.py:253
  29.5 0.3 collective-permute-start.10
  29.8 2.4 %collective-permute-start.8 = (bf16[32,8,1024]{2,1,0:T(8,128)(2,1)S(1)}, bf16[32,8,1024]{2,1,0:T(8,128)(2,1)S(1)}, u32[]{:S(2)}, u32[]{:S(2)}) collective-permute-start(bf16[32,8,1024]{2,1,0:T(8,128)(2,1)S(1)} %constant_dynamic-update-slice_fusion.4.refs_0_), channel_id=1, source_target_pairs={{0,6},{1,25},{2,0},{3,27},{4,2},{5,29},{6,4},{7,31},{8,14},{9,1},{... | collective-permute-start | bytes 1572872 | tf_op jit(solution)/shard_map/ppermute | solution.py:253
  32.2 0.8 %collective-permute-start.12 = (bf16[32,8,1024]{2,1,0:T(8,128)(2,1)S(1)}, bf16[32,8,1024]{2,1,0:T(8,128)(2,1)S(1)}, u32[]{:S(2)}, u32[]{:S(2)}) collective-permute-start(bf16[32,8,1024]{2,1,0:T(8,128)(2,1)S(1)} %constant_dynamic-update-slice_fusion.4.refs_0_), channel_id=1, source_target_pairs={{0,1},{1,0},{2,3},{3,2},{4,5},{5,4},{6,7},{7,6},{8,9},{9,8},{10,11... | collective-permute-start | bytes 1572872 | tf_op jit(solution)/shard_map/ppermute | solution.py:253
  33.0 3.7 %collective-permute-done.11.refs_3_ = bf16[32,8,1024]{2,1,0:T(8,128)(2,1)S(1)} collective-permute-done((bf16[32,8,1024]{2,1,0:T(8,128)(2,1)S(1)}, bf16[32,8,1024]{2,1,0:T(8,128)(2,1)S(1)}, u32[]{:S(2)}, u32[]{:S(2)}) %collective-permute-start.11) | collective-permute-done | bytes 524320 | tf_op jit(solution)/shard_map/ppermute | solution.py:253
  36.6 0.7 %collective-permute-start.13 = (bf16[32,8,1024]{2,1,0:T(8,128)(2,1)S(1)}, bf16[32,8,1024]{2,1,0:T(8,128)(2,1)S(1)}, u32[]{:S(2)}, u32[]{:S(2)}) collective-permute-start(bf16[32,8,1024]{2,1,0:T(8,128)(2,1)S(1)} %collective-permute-done.11.refs_3_), channel_id=1, source_target_pairs={{0,1},{1,0},{2,3},{3,2},{4,5},{5,4},{6,7},{7,6},{8,9},{9,8},{10,11... | collective-permute-start | bytes 1572872 | tf_op jit(solution)/shard_map/ppermute | solution.py:253
  37.3 4.9 %collective-permute-done.10.refs_2_ = bf16[32,8,1024]{2,1,0:T(8,128)(2,1)S(1)} collective-permute-done((bf16[32,8,1024]{2,1,0:T(8,128)(2,1)S(1)}, bf16[32,8,1024]{2,1,0:T(8,128)(2,1)S(1)}, u32[]{:S(2)}, u32[]{:S(2)}) %collective-permute-start.10) | collective-permute-done | bytes 524320 | tf_op jit(solution)/shard_map/ppermute | solution.py:253
  42.2 0.6 %collective-permute-start.14 = (bf16[32,8,1024]{2,1,0:T(8,128)(2,1)S(1)}, bf16[32,8,1024]{2,1,0:T(8,128)(2,1)S(1)}, u32[]{:S(2)}, u32[]{:S(2)}) collective-permute-start(bf16[32,8,1024]{2,1,0:T(8,128)(2,1)S(1)} %collective-permute-done.10.refs_2_), channel_id=1, source_target_pairs={{0,1},{1,0},{2,3},{3,2},{4,5},{5,4},{6,7},{7,6},{8,9},{9,8},{10,11... | collective-permute-start | bytes 1572872 | tf_op jit(solution)/shard_map/ppermute | solution.py:253
  42.9 0.4 collective-permute-start.9
  43.2 1.1 %collective-permute-done.14.refs_6_ = bf16[32,8,1024]{2,1,0:T(8,128)(2,1)S(1)} collective-permute-done((bf16[32,8,1024]{2,1,0:T(8,128)(2,1)S(1)}, bf16[32,8,1024]{2,1,0:T(8,128)(2,1)S(1)}, u32[]{:S(2)}, u32[]{:S(2)}) %collective-permute-start.14) | collective-permute-done | bytes 524320 | tf_op jit(solution)/shard_map/ppermute | solution.py:253
  44.4 1.4 %shard_map.43.early = f32[8,2048,128]{2,1,0:T(8,128)S(1)} custom-call(s32[8,32]{1,0:T(8,128)S(1)} %get-tuple-element.14.far_rows, bf16[32,8,1024]{2,1,0:T(8,128)(2,1)S(1)} %constant_dynamic-update-slice_fusion.4.refs_0_, bf16[32,8,1024]{2,1,0:T(8,128)(2,1)S(1)} %collective-permute-done.8.refs_1_, bf16[32,8,1024]{2,1,0:T(8,128)(2,1)S(1)} %collective-permute-done.10.refs_2_, ...), custom_call_target="tpu_custom_call" | custom-call | tf_op jit(solution)/shard_map/pallas_call | solution.py:216
  45.8 6.5 %shard_map.44 = (bf16[8,1536,512]{2,1,0:T(8,128)(2,1)}, bf16[8,4,12]{2,1,0:T(4,128)(2,1)}, f32[8,2048,128]{2,1,0:T(8,128)S(1)}) custom-call(s32[8,32]{1,0:T(8,128)S(1)} %get-tuple-element.14.far_rows, bf16[32,8,1024]{2,1,0:T(8,128)(2,1)S(1)} %collective-permute-done.9.late, f32[8,2048,128]{2,1,0:T(8,128)S(1)} %shard_map.43.early), custom_call_target="tpu_custom_call", output_to_operand_aliasing={{2}: (2, {})} | custom-call | flops 1610612736 | bytes 12582912 | tf_op jit(solution)/shard_map/pallas_call | solution.py:224
  (21 shorter events, 0.4 us)
Async XLA Ops:
  0.6 5.2 %collective-permute-start = (bf16[8,8,1024]{2,1,0:T(8,128)(2,1)}, bf16[8,8,1024]{2,1,0:T(8,128)(2,1)S(1)}, u32[]{:S(2)}, u32[]{:S(2)}) collective-permute-start(bf16[8,8,1024]{2,1,0:T(8,128)(2,1)} %bitcast.3), channel_id=1, source_target_pairs={{0,1},{1,0},{2,3},{3,2},{4,5},{5,4},{6,7},{7,6},{8,9},{9,8},{10,11... | collective-permute-start | bytes 393224 | tf_op jit(solution)/shard_map/ppermute | solution.py:253
  4.0 0.9 %copy-start = (bf16[1,1,8,8,1024]{4,3,2,1,0:T(8,128)(2,1)S(1)}, bf16[1,1,8,8,1024]{4,3,2,1,0:T(8,128)(2,1)}, u32[]{:S(2)}) copy-start(bf16[1,1,8,8,1024]{4,3,2,1,0:T(8,128)(2,1)} %param.2) | copy-start | bytes 393220
  4.9 0.8 %copy-start.1 = (s32[8,32,8,2]{1,3,2,0:T(2,128)S(1)}, s32[8,32,8,2]{1,3,2,0:T(2,128)}, u32[]{:S(2)}) copy-start(s32[8,32,8,2]{1,3,2,0:T(2,128)} %param.3) | copy-start | bytes 49156
  6.0 11.9 %collective-permute-start.1 = (bf16[2,8,1024]{2,1,0:T(8,128)(2,1)S(1)}, bf16[2,8,1024]{2,1,0:T(8,128)(2,1)S(1)}, u32[]{:S(2)}, u32[]{:S(2)}) collective-permute-start(bf16[2,8,1024]{2,1,0:T(8,128)(2,1)S(1)} %get-tuple-element.20), channel_id=1, source_target_pairs={{0,0},{1,129},{2,2},{3,131},{4,4},{5,133},{6,6},{7,135},{8,8},{9,1... | collective-permute-start | bytes 98312 | tf_op jit(solution)/shard_map/ppermute | solution.py:259
  13.0 4.9 %collective-permute-start.2 = (bf16[2,8,1024]{2,1,0:T(8,128)(2,1)S(1)}, bf16[2,8,1024]{2,1,0:T(8,128)(2,1)S(1)}, u32[]{:S(2)}, u32[]{:S(2)}) collective-permute-start(bf16[2,8,1024]{2,1,0:T(8,128)(2,1)S(1)} %get-tuple-element.21), channel_id=1, source_target_pairs={{0,32},{1,225},{2,34},{3,227},{4,36},{5,229},{6,38},{7,231},{8,40}... | collective-permute-start | bytes 98312 | tf_op jit(solution)/shard_map/ppermute | solution.py:259
  13.1 4.8 %collective-permute-start.3 = (bf16[2,8,1024]{2,1,0:T(8,128)(2,1)S(1)}, bf16[2,8,1024]{2,1,0:T(8,128)(2,1)S(1)}, u32[]{:S(2)}, u32[]{:S(2)}) collective-permute-start(bf16[2,8,1024]{2,1,0:T(8,128)(2,1)S(1)} %get-tuple-element.22), channel_id=1, source_target_pairs={{0,64},{1,193},{2,66},{3,195},{4,68},{5,197},{6,70},{7,199},{8,72}... | collective-permute-start | bytes 98312 | tf_op jit(solution)/shard_map/ppermute | solution.py:259
  13.2 5.7 %collective-permute-start.4 = (bf16[2,8,1024]{2,1,0:T(8,128)(2,1)S(1)}, bf16[2,8,1024]{2,1,0:T(8,128)(2,1)S(1)}, u32[]{:S(2)}, u32[]{:S(2)}) collective-permute-start(bf16[2,8,1024]{2,1,0:T(8,128)(2,1)S(1)} %get-tuple-element.23), channel_id=1, source_target_pairs={{0,96},{1,161},{2,98},{3,163},{4,100},{5,165},{6,102},{7,167},{8,1... | collective-permute-start | bytes 98312 | tf_op jit(solution)/shard_map/ppermute | solution.py:259
  18.9 5.4 %collective-permute-start.5 = (bf16[8,8,1024]{2,1,0:T(8,128)(2,1)S(1)}, bf16[8,8,1024]{2,1,0:T(8,128)(2,1)S(1)}, u32[]{:S(2)}, u32[]{:S(2)}) collective-permute-start(bf16[8,8,1024]{2,1,0:T(8,128)(2,1)S(1)} %get-tuple-element.26), channel_id=1, source_target_pairs={{0,8},{1,3},{2,10},{3,5},{4,12},{5,7},{6,14},{7,1},{8,16},{9,11},{... | collective-permute-start | bytes 393224 | tf_op jit(solution)/shard_map/ppermute | solution.py:253
  20.2 6.4 %collective-permute-start.6 = (bf16[8,8,1024]{2,1,0:T(8,128)(2,1)S(1)}, bf16[8,8,1024]{2,1,0:T(8,128)(2,1)S(1)}, u32[]{:S(2)}, u32[]{:S(2)}) collective-permute-start(bf16[8,8,1024]{2,1,0:T(8,128)(2,1)S(1)} %get-tuple-element.26), channel_id=1, source_target_pairs={{0,16},{1,5},{2,18},{3,7},{4,20},{5,1},{6,22},{7,3},{8,24},{9,13},... | collective-permute-start | bytes 393224 | tf_op jit(solution)/shard_map/ppermute | solution.py:253
  22.8 3.8 %collective-permute-start.7 = (bf16[8,8,1024]{2,1,0:T(8,128)(2,1)S(1)}, bf16[8,8,1024]{2,1,0:T(8,128)(2,1)S(1)}, u32[]{:S(2)}, u32[]{:S(2)}) collective-permute-start(bf16[8,8,1024]{2,1,0:T(8,128)(2,1)S(1)} %get-tuple-element.26), channel_id=1, source_target_pairs={{0,24},{1,7},{2,26},{3,1},{4,28},{5,3},{6,30},{7,5},{8,0},{9,15},{... | collective-permute-start | bytes 393224 | tf_op jit(solution)/shard_map/ppermute | solution.py:253
  26.7 10.0 %collective-permute-start.11 = (bf16[32,8,1024]{2,1,0:T(8,128)(2,1)S(1)}, bf16[32,8,1024]{2,1,0:T(8,128)(2,1)S(1)}, u32[]{:S(2)}, u32[]{:S(2)}) collective-permute-start(bf16[32,8,1024]{2,1,0:T(8,128)(2,1)S(1)} %constant_dynamic-update-slice_fusion.4.refs_0_), channel_id=1, source_target_pairs={{0,4},{1,17},{2,6},{3,19},{4,0},{5,21},{6,2},{7,23},{8,12},{9,25},... | collective-permute-start | bytes 1572872 | tf_op jit(solution)/shard_map/ppermute | solution.py:253
  29.5 12.7 %collective-permute-start.10 = (bf16[32,8,1024]{2,1,0:T(8,128)(2,1)S(1)}, bf16[32,8,1024]{2,1,0:T(8,128)(2,1)S(1)}, u32[]{:S(2)}, u32[]{:S(2)}) collective-permute-start(bf16[32,8,1024]{2,1,0:T(8,128)(2,1)S(1)} %constant_dynamic-update-slice_fusion.4.refs_0_), channel_id=1, source_target_pairs={{0,2},{1,9},{2,4},{3,11},{4,6},{5,13},{6,0},{7,15},{8,10},{9,17},{... | collective-permute-start | bytes 1572872 | tf_op jit(solution)/shard_map/ppermute | solution.py:253
  29.8 13.0 %collective-permute-start.8 = (bf16[32,8,1024]{2,1,0:T(8,128)(2,1)S(1)}, bf16[32,8,1024]{2,1,0:T(8,128)(2,1)S(1)}, u32[]{:S(2)}, u32[]{:S(2)}) collective-permute-start(bf16[32,8,1024]{2,1,0:T(8,128)(2,1)S(1)} %constant_dynamic-update-slice_fusion.4.refs_0_), channel_id=1, source_target_pairs={{0,6},{1,25},{2,0},{3,27},{4,2},{5,29},{6,4},{7,31},{8,14},{9,1},{... | collective-permute-start | bytes 1572872 | tf_op jit(solution)/shard_map/ppermute | solution.py:253
  32.2 11.1 %collective-permute-start.12 = (bf16[32,8,1024]{2,1,0:T(8,128)(2,1)S(1)}, bf16[32,8,1024]{2,1,0:T(8,128)(2,1)S(1)}, u32[]{:S(2)}, u32[]{:S(2)}) collective-permute-start(bf16[32,8,1024]{2,1,0:T(8,128)(2,1)S(1)} %constant_dynamic-update-slice_fusion.4.refs_0_), channel_id=1, source_target_pairs={{0,1},{1,0},{2,3},{3,2},{4,5},{5,4},{6,7},{7,6},{8,9},{9,8},{10,11... | collective-permute-start | bytes 1572872 | tf_op jit(solution)/shard_map/ppermute | solution.py:253
  36.6 6.6 %collective-permute-start.13 = (bf16[32,8,1024]{2,1,0:T(8,128)(2,1)S(1)}, bf16[32,8,1024]{2,1,0:T(8,128)(2,1)S(1)}, u32[]{:S(2)}, u32[]{:S(2)}) collective-permute-start(bf16[32,8,1024]{2,1,0:T(8,128)(2,1)S(1)} %collective-permute-done.11.refs_3_), channel_id=1, source_target_pairs={{0,1},{1,0},{2,3},{3,2},{4,5},{5,4},{6,7},{7,6},{8,9},{9,8},{10,11... | collective-permute-start | bytes 1572872 | tf_op jit(solution)/shard_map/ppermute | solution.py:253
  42.2 2.2 %collective-permute-start.14 = (bf16[32,8,1024]{2,1,0:T(8,128)(2,1)S(1)}, bf16[32,8,1024]{2,1,0:T(8,128)(2,1)S(1)}, u32[]{:S(2)}, u32[]{:S(2)}) collective-permute-start(bf16[32,8,1024]{2,1,0:T(8,128)(2,1)S(1)} %collective-permute-done.10.refs_2_), channel_id=1, source_target_pairs={{0,1},{1,0},{2,3},{3,2},{4,5},{5,4},{6,7},{7,6},{8,9},{9,8},{10,11... | collective-permute-start | bytes 1572872 | tf_op jit(solution)/shard_map/ppermute | solution.py:253
  42.9 3.0 %collective-permute-start.9 = (bf16[32,8,1024]{2,1,0:T(8,128)(2,1)S(1)}, bf16[32,8,1024]{2,1,0:T(8,128)(2,1)S(1)}, u32[]{:S(2)}, u32[]{:S(2)}) collective-permute-start(bf16[32,8,1024]{2,1,0:T(8,128)(2,1)S(1)} %collective-permute-done.8.refs_1_), channel_id=1, source_target_pairs={{0,1},{1,0},{2,3},{3,2},{4,5},{5,4},{6,7},{7,6},{8,9},{9,8},{10,11... | collective-permute-start | bytes 1572872 | tf_op jit(solution)/shard_map/ppermute | solution.py:253
